TPU v7x, 32 devices: a whole 2x2x4 slice. The times are simulated.
32 devices in a mesh: dp: 2 (over x), row: 4 (over y, core), col: 4 (over z).
Axes of the slice: x: 2, y: 2, z: 4, core: 2. Of those that a mesh axis runs over, the one named last changes fastest.
Arguments:
- images_in: bfloat16 [8, 640, 1024], P(('dp', 'col'), None, 'row'), may hold values from -6 to 6
- adapter_id: int32 [8], P('dp'), may hold values from 0 to 7
- valid_mask: int32 [8, 640], P('dp'), may hold values from 0 to 1, as said below
- ln1_gain: bfloat16 [1024], P('row'), may hold values from 0.25 to 1.75
- ln1_bias: bfloat16 [1024], P('row'), may hold values from -3 to 3
- qkv_weight: bfloat16 [3, 1024, 1024], P(None, 'row', 'col'), may hold values from -0.1875 to 0.1875
- qv_bias: bfloat16 [2, 1024], P(None, 'col'), may hold values from -3 to 3
- out_weight: bfloat16 [1024, 1024], P('col', 'row'), may hold values from -2 to 2
- out_bias: bfloat16 [1024], P('row'), may hold values from -3 to 3
- ln2_gain: bfloat16 [1024], P('row'), may hold values from 0.25 to 1.75
- ln2_bias: bfloat16 [1024], P('row'), may hold values from -3 to 3
- fc1_weight: bfloat16 [1024, 4096], P('row', 'col'), may hold values from -0.1875 to 0.1875
- fc1_bias: bfloat16 [4096], P('col'), may hold values from -3 to 3
- fc2_weight: bfloat16 [4096, 1024], P('col', 'row'), may hold values from -0.09375 to 0.09375
- fc2_bias: bfloat16 [1024], P('row'), may hold values from -3 to 3
- qkv_down: bfloat16 [3, 8, 1024, 16], P(None, None, 'row'), may hold values from -0.1875 to 0.1875
- qkv_up: bfloat16 [3, 8, 16, 1024], P(None, None, None, 'col'), may hold values from -1 to 1
- out_down: bfloat16 [8, 1024, 16], P(None, 'col'), may hold values from -2 to 2
- out_up: bfloat16 [8, 16, 1024], P(None, None, 'row'), may hold values from -1 to 1
- fc1_down: bfloat16 [8, 1024, 16], P(None, 'row'), may hold values from -0.1875 to 0.1875
- fc1_up: bfloat16 [8, 16, 4096], P(None, None, 'col'), may hold values from -1 to 1
- fc2_down: bfloat16 [8, 4096, 16], P(None, 'col'), may hold values from -0.09375 to 0.09375
- fc2_up: bfloat16 [8, 16, 1024], P(None, None, 'row'), may hold values from -1 to 1
- out_cotangent: bfloat16 [8, 640, 1024], P(('dp', 'col'), None, 'row'), may hold values from -6 to 6
Outputs:
- block_out: bfloat16 [8, 640, 1024], P(('dp', 'col'), None, 'row')
- input_grad: bfloat16 [8, 640, 1024], P(('dp', 'col'), None, 'row')
- qkv_down_grad: float32 [3, 8, 1024, 16], P(None, None, 'row')
- qkv_up_grad: float32 [3, 8, 16, 1024], P(None, None, None, 'col')
- out_down_grad: float32 [8, 1024, 16], P(None, 'col')
- out_up_grad: float32 [8, 16, 1024], P(None, None, 'row')
- fc1_down_grad: float32 [8, 1024, 16], P(None, 'row')
- fc1_up_grad: float32 [8, 16, 4096], P(None, None, 'col')
- fc2_down_grad: float32 [8, 4096, 16], P(None, 'col')
- fc2_up_grad: float32 [8, 16, 1024], P(None, None, 'row')
Inputs may be any that keep to these rules, and one draw needn't show every extreme that they name: `valid_mask`: the valid slots of an image are its first L slots, with 144 <= L <= 577; some image has exactly 577.
All inputs are finite; a program needn't handle non-finite values.
Results may differ from a plain program's by a relative error of at most 0.02.
Values may be sent and summed in bfloat16 or wider, within the bound.
A program may use at most 128 MiB of HBM per device.

v0:
```python
import jax
import jax.numpy as jnp
from jax import lax
from jax.sharding import PartitionSpec as P

HEAD_DIM = 64
RANK = 16
ADAPTERS = 8


MASKED_SCORE = -1e30
EPSILON = 1e-06
SQRT_HALF = 0.7071067811865476
INV_ROOT_TAU = 0.3989422804014327


def choose_table(labels):
    return (labels[:, None] == jnp.arange(ADAPTERS)[None, :]).astype(jnp.float32)


def pick_rank(projected, table):
    shaped = projected.reshape(projected.shape[:-1] + (ADAPTERS, RANK))
    return jnp.sum(shaped * table[:, None, None, :, None], axis=-2)


def spread_rank(low_values, table):
    spread = low_values[..., None, :] * table.astype(jnp.bfloat16)[:, None, None, :, None]
    return spread.reshape(low_values.shape[:-1] + (ADAPTERS * RANK,))


def down_columns(down_factor):
    reordered = jnp.transpose(down_factor, (2, 0, 1, 3))
    return reordered.reshape(reordered.shape[0], -1)[None]


def down_rows(down_factor):
    reordered = jnp.transpose(down_factor, (0, 1, 3, 2))
    return reordered.reshape(reordered.shape[0], ADAPTERS * RANK, reordered.shape[3])


def up_rows(up_factor):
    reordered = jnp.transpose(up_factor, (0, 3, 1, 2))
    return reordered.reshape(reordered.shape[0], reordered.shape[1], ADAPTERS * RANK)


def up_columns(up_factor):
    return up_factor.reshape(up_factor.shape[0], ADAPTERS * RANK, up_factor.shape[3])


def project(inputs, weights, adapter_in):
    dense_part = jnp.einsum("nskc,kcm->nsm", inputs, weights, preferred_element_type=jnp.float32)
    rank_part = jnp.einsum("nskc,kcf->nskf", inputs, adapter_in, preferred_element_type=jnp.float32)
    return jnp.concatenate([dense_part, rank_part.reshape(rank_part.shape[:2] + (-1,))], axis=-1)


def split_result(result, main_width, members):
    dense_part = result[..., :main_width]
    rank_part = result[..., main_width:].reshape(result.shape[:-1] + (members, ADAPTERS * RANK))
    return (dense_part, rank_part)


def rank_apply(low_values, table, factor, keep_members):
    formula = "nspf,pfm->nspm" if keep_members else "nspf,pfm->nsm"
    return jnp.einsum(
        formula, spread_rank(low_values, table), factor, preferred_element_type=jnp.float32
    )


def down_grad(inputs, grad_low, table):
    spread = spread_rank(grad_low, table).reshape(grad_low.shape[:-1] + (ADAPTERS, RANK))
    return jnp.einsum("nsd,nspar->padr", inputs, spread, preferred_element_type=jnp.float32)


def up_grad(low_values, incoming, table):
    spread = spread_rank(low_values, table).reshape(low_values.shape[:-1] + (ADAPTERS, RANK))
    return jnp.einsum("nspar,nspm->parm", spread, incoming, preferred_element_type=jnp.float32)


def row_totals(first, second):
    return lax.psum((first, second), "row")


def norm_forward(values, gain, bias, totals_of, width):
    first, second = totals_of(jnp.sum(values, axis=-1), jnp.sum(values * values, axis=-1))
    center = first / width
    spread = second / width - center * center
    scaling = lax.rsqrt(spread + EPSILON)
    normal = (values - center[..., None]) * scaling[..., None]
    return (normal * gain.astype(jnp.float32) + bias.astype(jnp.float32), normal, scaling)


def norm_backward(incoming, normal, scaling, gain, totals_of, width):
    scaled = incoming * gain.astype(jnp.float32)
    first, second = totals_of(jnp.sum(scaled, axis=-1), jnp.sum(scaled * normal, axis=-1))
    return scaling[..., None] * (
        scaled - first[..., None] / width - normal * second[..., None] / width
    )


def gelu_slope(hidden):
    lower = 0.5 * (1.0 + jax.scipy.special.erf(hidden * SQRT_HALF))
    return lower + hidden * jnp.exp(-0.5 * hidden * hidden) * INV_ROOT_TAU


def masked_scores(queries, key_rows, valid_keys):
    scores = jnp.einsum(
        "qhd,khd->hqk", queries, key_rows, preferred_element_type=jnp.float32
    ) * HEAD_DIM ** (-0.5)
    return jnp.where(valid_keys[None, None, :] > 0, scores, MASKED_SCORE)


def attend_image(operands):
    queries, key_rows, values, valid_keys = operands
    scores = masked_scores(queries, key_rows, valid_keys)
    highest = jnp.max(scores, axis=-1)
    powered = jnp.exp(scores - highest[..., None])
    summed = jnp.sum(powered, axis=-1)
    probabilities = (powered / summed[..., None]).astype(jnp.bfloat16)
    attended = jnp.einsum("hqk,khd->qhd", probabilities, values, preferred_element_type=jnp.float32)
    return (attended, highest + jnp.log(summed))


def attend_back(operands):
    queries, key_rows, values, valid_keys, log_totals, grad_out = operands
    scores = masked_scores(queries, key_rows, valid_keys)
    probabilities = jnp.exp(scores - log_totals[..., None])
    grad_values = jnp.einsum(
        "hqk,qhd->khd",
        probabilities.astype(jnp.bfloat16),
        grad_out,
        preferred_element_type=jnp.float32,
    )
    grad_probs = jnp.einsum("qhd,khd->hqk", grad_out, values, preferred_element_type=jnp.float32)
    inner = jnp.sum(probabilities * grad_probs, axis=-1, keepdims=True)
    grad_scores = (probabilities * (grad_probs - inner)).astype(jnp.bfloat16)
    grad_queries = jnp.einsum(
        "hqk,khd->qhd", grad_scores, key_rows, preferred_element_type=jnp.float32
    ) * HEAD_DIM ** (-0.5)
    grad_keys = jnp.einsum(
        "hqk,qhd->khd", grad_scores, queries, preferred_element_type=jnp.float32
    ) * HEAD_DIM ** (-0.5)
    return (grad_queries, grad_keys, grad_values)


def grid_attention(valid_rows):

    def forward(qkv_low_b):
        images, slot_count = (qkv_low_b.shape[0], qkv_low_b.shape[1])
        shaped = qkv_low_b.reshape(images, slot_count, 3, -1, HEAD_DIM)
        saved = (shaped[:, :, 0], shaped[:, :, 1], shaped[:, :, 2])
        attended, log_totals = lax.map(attend_image, saved + (valid_rows,))
        return (
            attended.reshape(images, slot_count, -1).astype(jnp.bfloat16),
            saved + (log_totals,),
        )

    def backward(saved, grad_context):
        queries, key_rows, values, log_totals = saved
        grad_out = grad_context.reshape(queries.shape)
        grad_queries, grad_keys, grad_values = lax.map(
            attend_back, (queries, key_rows, values, valid_rows, log_totals, grad_out)
        )
        stacked = jnp.stack([grad_queries, grad_keys, grad_values], axis=2)
        return stacked.reshape(queries.shape[0], queries.shape[1], 3, -1).astype(jnp.bfloat16)

    return (forward, backward)


def into_rows(inputs, weights, adapter_in):
    gathered = lax.all_gather(inputs, "col", axis=0, tiled=True)
    share = gathered.shape[0] // lax.axis_size("row")

    def term(offset, amount):
        return project(gathered, weights, adapter_in)

    return lax.psum_scatter(
        term(jnp.int32(0), share * lax.axis_size("row")), "row", scatter_dimension=0, tiled=True
    )


def into_columns(inputs, weights, adapter_in):

    def term(portion, offset):
        return project(portion, weights, adapter_in)

    partial_sums = term(lax.all_gather(inputs, "row", axis=0, tiled=True), jnp.int32(0))
    return lax.psum_scatter(
        partial_sums.astype(jnp.bfloat16), "col", scatter_dimension=0, tiled=True
    ).astype(jnp.float32)


def run_block(residual_in, cotangent, tables, params, adapters, moves, totals_of, attention, width):
    table_first, table_second = tables
    to_second, to_first = moves
    attend_forward, attend_backward = attention
    (
        gain_one,
        bias_one,
        qkv_weight,
        qv_bias,
        out_weight,
        out_bias,
        gain_two,
        bias_two,
        fc1_weight,
        fc1_bias,
        fc2_weight,
        fc2_bias,
    ) = params
    qkv_down, qkv_up, out_down, out_up, fc1_down, fc1_up, fc2_down, fc2_up = adapters
    first_cols = residual_in.shape[2]
    head_cols = qkv_weight.shape[2]
    hidden_cols = fc1_weight.shape[1]
    residual = residual_in.astype(jnp.float32)
    norm_one, normal_one, scaling_one = norm_forward(residual, gain_one, bias_one, totals_of, width)
    norm_one_b = norm_one.astype(jnp.bfloat16)
    merged_qkv = jnp.transpose(qkv_weight, (1, 0, 2)).reshape(qkv_weight.shape[1], 3 * head_cols)[
        None
    ]
    dense_part, rank_part = split_result(
        to_second(norm_one_b[:, :, None, :], merged_qkv, down_columns(qkv_down)), 3 * head_cols, 3
    )
    qkv_low = pick_rank(rank_part, table_second).astype(jnp.bfloat16)
    qkv_bias = jnp.stack([qv_bias[0], jnp.zeros_like(qv_bias[0]), qv_bias[1]]).astype(jnp.float32)
    qkv_values = (
        dense_part.reshape(dense_part.shape[:2] + (3, head_cols))
        + qkv_bias
        + rank_apply(qkv_low, table_second, up_columns(qkv_up), True)
    )
    qkv_low_b = qkv_values.astype(jnp.bfloat16)
    context_b, saved = attend_forward(qkv_low_b)
    dense_part, rank_part = split_result(
        to_first(context_b[:, :, None, :], out_weight[None], down_columns(out_down[None])),
        first_cols,
        1,
    )
    out_low = pick_rank(rank_part, table_first).astype(jnp.bfloat16)
    mixed = (
        residual
        + dense_part
        + out_bias.astype(jnp.float32)
        + rank_apply(out_low, table_first, up_columns(out_up[None]), False)
    )
    norm_two, normal_two, scaling_two = norm_forward(mixed, gain_two, bias_two, totals_of, width)
    norm_two_b = norm_two.astype(jnp.bfloat16)
    dense_part, rank_part = split_result(
        to_second(norm_two_b[:, :, None, :], fc1_weight[None], down_columns(fc1_down[None])),
        hidden_cols,
        1,
    )
    fc1_low = pick_rank(rank_part, table_second).astype(jnp.bfloat16)
    hidden = (
        dense_part
        + fc1_bias.astype(jnp.float32)
        + rank_apply(fc1_low, table_second, up_columns(fc1_up[None]), False)
    )
    activated_b = jax.nn.gelu(hidden, approximate=False).astype(jnp.bfloat16)
    dense_part, rank_part = split_result(
        to_first(activated_b[:, :, None, :], fc2_weight[None], down_columns(fc2_down[None])),
        first_cols,
        1,
    )
    fc2_low = pick_rank(rank_part, table_first).astype(jnp.bfloat16)
    block_out = (
        mixed
        + dense_part
        + fc2_bias.astype(jnp.float32)
        + rank_apply(fc2_low, table_first, up_columns(fc2_up[None]), False)
    ).astype(jnp.bfloat16)
    dense_part, rank_part = split_result(
        to_second(cotangent[:, :, None, :], jnp.transpose(fc2_weight)[None], up_rows(fc2_up[None])),
        hidden_cols,
        1,
    )
    fc2_grad_low = pick_rank(rank_part, table_second).astype(jnp.bfloat16)
    grad_activated = dense_part + rank_apply(
        fc2_grad_low, table_second, down_rows(fc2_down[None]), False
    )
    fc2_down_part = down_grad(activated_b, fc2_grad_low, table_second)[0]
    fc2_up_part = up_grad(fc2_low, cotangent[:, :, None, :], table_first)[0]
    grad_hidden_b = (grad_activated * gelu_slope(hidden)).astype(jnp.bfloat16)
    dense_part, rank_part = split_result(
        to_first(
            grad_hidden_b[:, :, None, :], jnp.transpose(fc1_weight)[None], up_rows(fc1_up[None])
        ),
        first_cols,
        1,
    )
    fc1_grad_low = pick_rank(rank_part, table_first).astype(jnp.bfloat16)
    grad_norm_two = dense_part + rank_apply(
        fc1_grad_low, table_first, down_rows(fc1_down[None]), False
    )
    fc1_down_part = down_grad(norm_two_b, fc1_grad_low, table_first)[0]
    fc1_up_part = up_grad(fc1_low, grad_hidden_b[:, :, None, :], table_second)[0]
    grad_mixed = cotangent.astype(jnp.float32) + norm_backward(
        grad_norm_two, normal_two, scaling_two, gain_two, totals_of, width
    )
    grad_branch_b = grad_mixed.astype(jnp.bfloat16)
    dense_part, rank_part = split_result(
        to_second(
            grad_branch_b[:, :, None, :], jnp.transpose(out_weight)[None], up_rows(out_up[None])
        ),
        head_cols,
        1,
    )
    out_grad_low = pick_rank(rank_part, table_second).astype(jnp.bfloat16)
    grad_context_b = (
        dense_part + rank_apply(out_grad_low, table_second, down_rows(out_down[None]), False)
    ).astype(jnp.bfloat16)
    out_down_part = down_grad(context_b, out_grad_low, table_second)[0]
    out_up_part = up_grad(out_low, grad_branch_b[:, :, None, :], table_first)[0]
    grad_qkv_b = attend_backward(saved, grad_context_b)
    dense_part, rank_part = split_result(
        to_first(grad_qkv_b, jnp.transpose(qkv_weight, (0, 2, 1)), up_rows(qkv_up)), first_cols, 3
    )
    qkv_grad_low = pick_rank(rank_part, table_first).astype(jnp.bfloat16)
    grad_norm_one = dense_part + rank_apply(qkv_grad_low, table_first, down_rows(qkv_down), False)
    qkv_down_part = down_grad(norm_one_b, qkv_grad_low, table_first)
    qkv_up_part = up_grad(qkv_low, grad_qkv_b, table_second)
    grad_input = grad_mixed + norm_backward(
        grad_norm_one, normal_one, scaling_one, gain_one, totals_of, width
    )
    return (
        block_out,
        grad_input.astype(jnp.bfloat16),
        (
            qkv_down_part,
            qkv_up_part,
            out_down_part,
            out_up_part,
            fc1_down_part,
            fc1_up_part,
            fc2_down_part,
            fc2_up_part,
        ),
    )


def grid_program(images_in, adapter_id, valid_mask, params, adapters, out_cotangent):
    row_index = lax.axis_index("row")
    col_index = lax.axis_index("col")
    local_images = images_in.shape[0]
    row_share = local_images * lax.axis_size("col") // lax.axis_size("row")
    labels_first = lax.dynamic_slice_in_dim(adapter_id, col_index * local_images, local_images, 0)
    labels_second = lax.dynamic_slice_in_dim(adapter_id, row_index * row_share, row_share, 0)
    valid_second = lax.dynamic_slice_in_dim(valid_mask, row_index * row_share, row_share, 0)
    block_out, grad_input, partials = run_block(
        images_in,
        out_cotangent,
        (choose_table(labels_first), choose_table(labels_second)),
        params,
        adapters,
        (into_rows, into_columns),
        row_totals,
        grid_attention(valid_second),
        images_in.shape[2] * lax.axis_size("row"),
    )
    (
        qkv_down_part,
        qkv_up_part,
        out_down_part,
        out_up_part,
        fc1_down_part,
        fc1_up_part,
        fc2_down_part,
        fc2_up_part,
    ) = partials
    width_sums = lax.psum((qkv_down_part, out_up_part, fc1_down_part, fc2_up_part), ("dp", "col"))
    other_sums = lax.psum((qkv_up_part, out_down_part, fc1_up_part, fc2_down_part), ("dp", "row"))
    return (
        block_out,
        grad_input,
        width_sums[0],
        other_sums[0],
        other_sums[1],
        width_sums[1],
        width_sums[2],
        other_sums[2],
        other_sums[3],
        width_sums[3],
    )


def shards(
    images_in,
    adapter_id,
    valid_mask,
    ln1_gain,
    ln1_bias,
    qkv_weight,
    qv_bias,
    out_weight,
    out_bias,
    ln2_gain,
    ln2_bias,
    fc1_weight,
    fc1_bias,
    fc2_weight,
    fc2_bias,
    qkv_down,
    qkv_up,
    out_down,
    out_up,
    fc1_down,
    fc1_up,
    fc2_down,
    fc2_up,
    out_cotangent,
):
    params = (
        ln1_gain,
        ln1_bias,
        qkv_weight,
        qv_bias,
        out_weight,
        out_bias,
        ln2_gain,
        ln2_bias,
        fc1_weight,
        fc1_bias,
        fc2_weight,
        fc2_bias,
    )
    adapters = (qkv_down, qkv_up, out_down, out_up, fc1_down, fc1_up, fc2_down, fc2_up)
    return grid_program(images_in, adapter_id, valid_mask, params, adapters, out_cotangent)


def solution(mesh):
    placed = (
        P(("dp", "col"), None, "row"),
        P("dp"),
        P("dp", None),
        P("row"),
        P("row"),
        P(None, "row", "col"),
        P(None, "col"),
        P("col", "row"),
        P("row"),
        P("row"),
        P("row"),
        P("row", "col"),
        P("col"),
        P("col", "row"),
        P("row"),
        P(None, None, "row", None),
        P(None, None, None, "col"),
        P(None, "col", None),
        P(None, None, "row"),
        P(None, "row", None),
        P(None, None, "col"),
        P(None, "col", None),
        P(None, None, "row"),
        P(("dp", "col"), None, "row"),
    )
    return jax.shard_map(
        shards,
        mesh=mesh,
        in_specs=placed,
        out_specs=(
            P(("dp", "col"), None, "row"),
            P(("dp", "col"), None, "row"),
            P(None, None, "row", None),
            P(None, None, None, "col"),
            P(None, "col", None),
            P(None, None, "row"),
            P(None, "row", None),
            P(None, None, "col"),
            P(None, "col", None),
            P(None, None, "row"),
        ),
        check_vma=False,
    )
```

profile of v0, /device:TPU:0, one launch (start us, length us, event | category | flops | bytes accessed | tf_op | source)
XLA Modules:
  0.0 1056.3 jit_solution(5152869188694253232)
XLA Ops:
  10.0 8.5 all-reduce.5
  19.9 32.9 %all-gather.19.cloned.1.call-done = bf16[4,640,256]{2,1,0:T(8,128)(2,1)} async-done(((bf16[1,640,256]{2,1,0:T(8,128)(2,1)}), bf16[4,640,256]{2,1,0:T(8,128)(2,1)}) %all-gather.19.cloned.1.call-update) | async-done | bytes 1310736 | tf_op jit(solution)/shard_map/all_gather | solution.py:170
  61.2 9.5 pad_maximum_fusion
  74.4 89.4 %reduce-scatter.9.cloned.1.call-done = f32[1,640,1152]{2,1,0:T(8,128)} async-done(((f32[4,640,1152]{2,1,0:T(8,128)}), f32[1,640,1152]{2,1,0:T(8,128)}) %reduce-scatter.9.cloned.1.call-update) | async-done | bytes 2949136 | tf_op jit(solution)/shard_map/reduce_scatter | solution.py:176
  179.0 18.3 %all-gather.15.cloned.1.call-done = bf16[4,640,1,256]{3,1,2,0:T(8,128)(2,1)} async-done(((bf16[1,640,1,256]{3,1,2,0:T(8,128)(2,1)}), bf16[4,640,1,256]{3,1,2,0:T(8,128)(2,1)}) %all-gather.15.cloned.1.call-update) | async-done | bytes 1310736 | tf_op jit(solution)/shard_map/all_gather | solution.py:186
  202.8 40.2 %reduce-scatter.11.cloned.1.call-done = bf16[1,640,384]{1,2,0:T(8,128)(2,1)} async-done(((bf16[4,640,384]{1,2,0:T(8,128)(2,1)}), bf16[1,640,384]{1,2,0:T(8,128)(2,1)}) %reduce-scatter.11.cloned.1.call-update) | async-done | bytes 491536 | tf_op jit(solution)/shard_map/reduce_scatter | solution.py:187
  245.6 6.6 all-reduce.4
  253.6 22.8 %all-gather.25.cloned.1.call-done = bf16[4,640,256]{2,1,0:T(8,128)(2,1)} async-done(((bf16[1,640,256]{2,1,0:T(8,128)(2,1)}), bf16[4,640,256]{2,1,0:T(8,128)(2,1)}) %all-gather.25.cloned.1.call-update) | async-done | bytes 1310736 | tf_op jit(solution)/shard_map/all_gather | solution.py:170
  283.8 9.6 pad_maximum_fusion.2
  293.5 16.6 %all-gather.21.cloned.1.call-done = bf16[4,640,256]{2,1,0:T(8,128)(2,1)} async-done(((bf16[1,640,256]{2,1,0:T(8,128)(2,1)}), bf16[4,640,256]{2,1,0:T(8,128)(2,1)}) %all-gather.21.cloned.1.call-update) | async-done | bytes 1310736 | tf_op jit(solution)/shard_map/all_gather | solution.py:170
  318.0 12.8 %pad_maximum_fusion.1 = f32[4,640,1152]{2,1,0:T(8,128)} fusion(f32[4,640,128]{2,1,0:T(8,128)S(1)} %fusion.129, f32[4,640,1024]{2,1,0:T(8,128)} %fusion.76), kind=kLoop, calls=%fused_computation.1 | loop fusion | flops 2949120 | bytes 23592960 | tf_op jit(solution)/shard_map/concatenate | solution.py:53
  331.6 74.1 %reduce-scatter.17.cloned.1.call-done = f32[1,640,1152]{2,1,0:T(8,128)} async-done(((f32[4,640,1152]{2,1,0:T(8,128)}), f32[1,640,1152]{2,1,0:T(8,128)}) %reduce-scatter.17.cloned.1.call-update) | async-done | bytes 2949136 | tf_op jit(solution)/shard_map/reduce_scatter | solution.py:176
  406.8 95.4 %reduce-scatter.13.cloned.1.call-done = f32[1,640,1152]{2,1,0:T(8,128)} async-done(((f32[4,640,1152]{2,1,0:T(8,128)}), f32[1,640,1152]{2,1,0:T(8,128)}) %reduce-scatter.13.cloned.1.call-update) | async-done | bytes 2949136 | tf_op jit(solution)/shard_map/reduce_scatter | solution.py:176
  503.7 8.9 fusion.10
  515.5 40.0 %all-gather.27.cloned.1.call-done = bf16[4,640,1024]{2,1,0:T(8,128)(2,1)} async-done(((bf16[1,640,1024]{2,1,0:T(8,128)(2,1)}), bf16[4,640,1024]{2,1,0:T(8,128)(2,1)}) %all-gather.27.cloned.1.call-update) | async-done | bytes 5242896 | tf_op jit(solution)/shard_map/all_gather | solution.py:186
  563.3 34.0 %all-gather.23.cloned.1.call-done = bf16[4,640,1024]{2,1,0:T(8,128)(2,1)} async-done(((bf16[1,640,1024]{2,1,0:T(8,128)(2,1)}), bf16[4,640,1024]{2,1,0:T(8,128)(2,1)}) %all-gather.23.cloned.1.call-update) | async-done | bytes 5242896 | tf_op jit(solution)/shard_map/all_gather | solution.py:186
  605.3 35.9 %reduce-scatter.19.cloned.1.call-done = bf16[1,640,384]{1,2,0:T(8,128)(2,1)} async-done(((bf16[4,640,384]{1,2,0:T(8,128)(2,1)}), bf16[1,640,384]{1,2,0:T(8,128)(2,1)}) %reduce-scatter.19.cloned.1.call-update) | async-done | bytes 491536 | tf_op jit(solution)/shard_map/reduce_scatter | solution.py:187
  642.1 41.9 %reduce-scatter.15.cloned.1.call-done = bf16[1,640,384]{1,2,0:T(8,128)(2,1)} async-done(((bf16[4,640,384]{1,2,0:T(8,128)(2,1)}), bf16[1,640,384]{1,2,0:T(8,128)(2,1)}) %reduce-scatter.15.cloned.1.call-update) | async-done | bytes 491536 | tf_op jit(solution)/shard_map/reduce_scatter | solution.py:187
  695.3 31.6 %all-gather.29.cloned.1.call-done = bf16[4,640,256]{2,1,0:T(8,128)(2,1)} async-done(((bf16[1,640,256]{2,1,0:T(8,128)(2,1)}), bf16[4,640,256]{2,1,0:T(8,128)(2,1)}) %all-gather.29.cloned.1.call-update) | async-done | bytes 1310736 | tf_op jit(solution)/shard_map/all_gather | solution.py:170
  733.7 40.8 %reduce-scatter.21.cloned.1.call-done = f32[1,640,384]{1,2,0:T(8,128)} async-done(((f32[4,640,384]{1,2,0:T(8,128)}), f32[1,640,384]{1,2,0:T(8,128)}) %reduce-scatter.21.cloned.1.call-update) | async-done | bytes 983056 | tf_op jit(solution)/shard_map/reduce_scatter | solution.py:176
  791.5 32.9 %all-gather.17.cloned.1.call-done = bf16[4,640,3,256]{3,1,2,0:T(8,128)(2,1)} async-done(((bf16[1,640,3,256]{3,1,2,0:T(8,128)(2,1)}), bf16[4,640,3,256]{3,1,2,0:T(8,128)(2,1)}) %all-gather.17.cloned.1.call-update) | async-done | bytes 3932176 | tf_op jit(solution)/shard_map/all_gather | solution.py:186
  845.5 49.1 %reduce-scatter.23.cloned.1.call-done = bf16[1,640,640]{1,2,0:T(8,128)(2,1)} async-done(((bf16[4,640,640]{1,2,0:T(8,128)(2,1)}), bf16[1,640,640]{1,2,0:T(8,128)(2,1)}) %reduce-scatter.23.cloned.1.call-update) | async-done | bytes 819216 | tf_op jit(solution)/shard_map/reduce_scatter | solution.py:187
  911.0 48.2 %all-reduce.11.cloned.1.call-done = (f32[3,8,16,256]{3,2,1,0:T(8,128)}, f32[8,256,16]{1,2,0:T(8,128)}, f32[8,16,1024]{2,1,0:T(8,128)}, f32[8,1024,16]{1,2,0:T(8,128)}) async-done(((f32[3,8,16,256]{3,2,1,0:T(8,128)}, f32[8,256,16]{1,2,0:T(8,128)}, f32[8,16,1024]{2,1,0:T(8,128)}, f32[8,1024,16]{1,2,0:T(8,128)}), (f32[3,8,16,256]{3,2,1,0:T(8,128)}, f32[8,256,16]{1,2,0:T(8,128)}, f32[8,16,1024]{2,1,0:T(8,128)}, ...) | async-done | bytes 1572880 | tf_op jit(solution)/shard_map/psum | solution.py:369
  959.2 79.3 %all-reduce.9.cloned.1.call-done = (f32[3,8,256,16]{2,3,1,0:T(8,128)}, f32[8,16,256]{2,1,0:T(8,128)}, f32[8,256,16]{1,2,0:T(8,128)}, f32[8,16,256]{2,1,0:T(8,128)}) async-done(((f32[3,8,256,16]{2,3,1,0:T(8,128)}, f32[8,16,256]{2,1,0:T(8,128)}, f32[8,256,16]{1,2,0:T(8,128)}, f32[8,16,256]{2,1,0:T(8,128)}), (f32[3,8,256,16]{2,3,1,0:T(8,128)}, f32[8,16,256]{2,1,0:T(8,128)}, f32[8,256,16]{1,2,0:T(8,128)}, ...) | async-done | bytes 786448 | tf_op jit(solution)/shard_map/psum | solution.py:368
  (358 shorter events, 160.9 us)
Async XLA Ops:
  7.2 304.9 %copy-start = (bf16[256,1024]{1,0:T(8,128)(2,1)S(1)}, bf16[256,1024]{1,0:T(8,128)(2,1)}, u32[]{:S(2)}) copy-start(bf16[256,1024]{1,0:T(8,128)(2,1)} %param.35) | copy-start | bytes 1572868
  7.2 45.6 %all-gather.19.cloned.1.call-start = ((), (), s32[]{:S(2)}) async-start(), calls=%async_computation.18 | async-start | bytes 1638400 | tf_op jit(solution)/shard_map/all_gather | solution.py:170
  8.5 236.7 %copy-start.3 = (bf16[1,640,256]{1,2,0:T(8,128)(2,1)}, bf16[1,640,256]{1,2,0:T(8,128)(2,1)S(1)}, u32[]{:S(2)}) copy-start(bf16[1,640,256]{1,2,0:T(8,128)(2,1)S(1)} %copy.113) | copy-start | bytes 983044
  19.6 144.2 %reduce-scatter.9.cloned.1.call-start = ((), (), s32[]{:S(2)}) async-start(), calls=%async_computation.8 | async-start | bytes 14745600 | tf_op jit(solution)/shard_map/reduce_scatter | solution.py:176
  70.8 126.5 %all-gather.15.cloned.1.call-start = ((), (), s32[]{:S(2)}) async-start(), calls=%async_computation.9 | async-start | bytes 1638400 | tf_op jit(solution)/shard_map/all_gather | solution.py:186
  72.7 430.9 %copy-start.66 = (bf16[8]{0:T(256)(128)(2,1)}, bf16[8]{0:T(256)(128)(2,1)S(1)}, u32[]{:S(2)}) copy-start(bf16[8]{0:T(256)(128)(2,1)S(1)} %fusion.118) | copy-start | bytes 52
  74.3 429.1 %copy-start.73 = (f32[8]{0:T(128)}, f32[8]{0:T(128)S(1)}, u32[]{:S(2)}) copy-start(f32[8]{0:T(128)S(1)} %compare_convert_fusion.1) | copy-start | bytes 100
  179.0 64.1 %reduce-scatter.11.cloned.1.call-start = ((), (), s32[]{:S(2)}) async-start(), calls=%async_computation.10 | async-start | bytes 2457600 | tf_op jit(solution)/shard_map/reduce_scatter | solution.py:187
  201.4 75.0 %all-gather.25.cloned.1.call-start = ((), (), s32[]{:S(2)}) async-start(), calls=%async_computation.21 | async-start | bytes 1638400 | tf_op jit(solution)/shard_map/all_gather | solution.py:170
  202.0 108.1 %all-gather.21.cloned.1.call-start = ((), (), s32[]{:S(2)}) async-start(), calls=%async_computation.19 | async-start | bytes 1638400 | tf_op jit(solution)/shard_map/all_gather | solution.py:170
  202.8 482.1 %copy-start.71 = (f32[8]{0:T(128)}, f32[8]{0:T(128)S(1)}, u32[]{:S(2)}) copy-start(f32[8]{0:T(128)S(1)} %get-tuple-element.116) | copy-start | bytes 100
  202.8 482.2 %copy-start.64 = (bf16[8]{0:T(256)(128)(2,1)}, bf16[8]{0:T(256)(128)(2,1)S(1)}, u32[]{:S(2)}) copy-start(bf16[8]{0:T(256)(128)(2,1)S(1)} %get-tuple-element.117) | copy-start | bytes 52
  253.4 152.3 %reduce-scatter.17.cloned.1.call-start = ((), (), s32[]{:S(2)}) async-start(), calls=%async_computation.13 | async-start | bytes 14745600 | tf_op jit(solution)/shard_map/reduce_scatter | solution.py:176
  293.5 208.8 %reduce-scatter.13.cloned.1.call-start = ((), (), s32[]{:S(2)}) async-start(), calls=%async_computation.11 | async-start | bytes 14745600 | tf_op jit(solution)/shard_map/reduce_scatter | solution.py:176
  330.9 224.5 %all-gather.27.cloned.1.call-start = ((), (), s32[]{:S(2)}) async-start(), calls=%async_computation.22 | async-start | bytes 6553600 | tf_op jit(solution)/shard_map/all_gather | solution.py:186
  514.8 82.5 %all-gather.23.cloned.1.call-start = ((), (), s32[]{:S(2)}) async-start(), calls=%async_computation.20 | async-start | bytes 6553600 | tf_op jit(solution)/shard_map/all_gather | solution.py:186
  515.4 125.7 %reduce-scatter.19.cloned.1.call-start = ((), (), s32[]{:S(2)}) async-start(), calls=%async_computation.14 | async-start | bytes 2457600 | tf_op jit(solution)/shard_map/reduce_scatter | solution.py:187
  563.0 121.0 %reduce-scatter.15.cloned.1.call-start = ((), (), s32[]{:S(2)}) async-start(), calls=%async_computation.12 | async-start | bytes 2457600 | tf_op jit(solution)/shard_map/reduce_scatter | solution.py:187
  605.0 121.9 %all-gather.29.cloned.1.call-start = ((), (), s32[]{:S(2)}) async-start(), calls=%async_computation.23 | async-start | bytes 1638400 | tf_op jit(solution)/shard_map/all_gather | solution.py:170
  695.2 79.2 %reduce-scatter.21.cloned.1.call-start = ((), (), s32[]{:S(2)}) async-start(), calls=%async_computation.15 | async-start | bytes 4915200 | tf_op jit(solution)/shard_map/reduce_scatter | solution.py:176
  732.4 91.9 %all-gather.17.cloned.1.call-start = ((), (), s32[]{:S(2)}) async-start(), calls=%async_computation.16 | async-start | bytes 4915200 | tf_op jit(solution)/shard_map/all_gather | solution.py:186
  791.2 103.5 %reduce-scatter.23.cloned.1.call-start = ((), (), s32[]{:S(2)}) async-start(), calls=%async_computation.17 | async-start | bytes 4096000 | tf_op jit(solution)/shard_map/reduce_scatter | solution.py:187
  832.2 127.0 %all-reduce.11.cloned.1.call-start = ((), (), s32[]{:S(2)}) async-start(), calls=%async_computation.25 | async-start | bytes 3145728 | tf_op jit(solution)/shard_map/psum | solution.py:369
  843.6 194.9 %all-reduce.9.cloned.1.call-start = ((), (), s32[]{:S(2)}) async-start(), calls=%async_computation.24 | async-start | bytes 1572864 | tf_op jit(solution)/shard_map/psum | solution.py:368
  (87 other events, 1375.3 us)
Sparse Core Ops, SparseCore 0:
  19.7 32.9 all-gather.18
  70.9 92.8 reduce-scatter.8
  179.1 18.1 all-gather.14
  201.6 41.4 reduce-scatter.10
  244.5 31.9 all-gather.24
  278.4 31.6 all-gather.20
  312.8 92.8 reduce-scatter.16
  408.3 93.8 reduce-scatter.12
  515.0 40.4 all-gather.26
  556.8 40.4 all-gather.22
  599.6 41.4 reduce-scatter.18
  643.3 40.6 reduce-scatter.14
  695.4 31.4 all-gather.28
  732.6 41.8 reduce-scatter.20
  791.3 32.9 all-gather.16
  832.3 62.2 reduce-scatter.22
  899.7 59.5 all-reduce.10
  963.9 74.5 all-reduce.8
where the time goes:
time: 1070 us; the launch traced here: 1060 us
  waiting for transfers between devices  825 us (77%)
  matrix products  88.7 us (8%)
  other arithmetic  55.6 us (5%)
  local copies, waits for them, and re-layouts  41.7 us (4%)
  blocking collectives  28.1 us (3%)
  between operations  16.2 us (2%)
    reduce_scatter x4, waiting for transfers between devices, into_rows(): lax.psum_scatter(term(jnp.int32(0), share * lax.axis_size('row')), 'row',...  300 us
    reduce_scatter x4, waiting for transfers between devices, into_columns(): lax.psum_scatter(partial_sums.astype(jnp.bfloat16), 'col', scatter_dimens...  167 us
    all_gather x4, waiting for transfers between devices, into_columns(): lax.all_gather(inputs, 'row', axis=0, tiled=True)  125 us
    all_gather x4, waiting for transfers between devices, into_rows(): gathered = lax.all_gather(inputs, 'col', axis=0, tiled=True)  104 us
    psum x1, waiting for transfers between devices, grid_program(): lax.psum((qkv_down_part, out_up_part, fc1_down_part, fc2_up_part), ('dp',...  79.3 us
    psum x1, waiting for transfers between devices, grid_program(): lax.psum((qkv_up_part, out_down_part, fc1_up_part, fc2_down_part), ('dp',...  48.2 us
    concatenate x8, other arithmetic, project(): jnp.concatenate([dense_part, rank_part.reshape(rank_part.shape[:2] + (-1,...  40.5 us
    psum x4, blocking collectives, row_totals(): return lax.psum((first, second), 'row')  28.1 us
  transfers between devices with their start and end apart: 18, of which 18 were waited for; matrix products, arithmetic and copies ran while one was open for 8% of the time, Pallas kernels for 0%

commit v1 on v0

v1 whole, which is shorter than its diff:
```python
import functools

import jax
import jax.numpy as jnp
from jax import lax
from jax.experimental import pallas as pl
from jax.experimental.pallas import tpu as pltpu
from jax.sharding import PartitionSpec as P

HEAD_DIM = 64
RANK = 16
ADAPTERS = 8
MASKED_SCORE = -1e30
EPSILON = 1e-06
SQRT_HALF = 0.7071067811865476
INV_ROOT_TAU = 0.3989422804014327

F32 = jnp.float32
BF16 = jnp.bfloat16
MESH = pl.DeviceIdType.MESH
VM = pltpu.VMEM
STEP = 32
PIECES = (1, 1, 2, 2)


def nn(a, b):
    return lax.dot_general(a, b, (((1,), (0,)), ((), ())), preferred_element_type=F32)


def nt(a, b):
    return lax.dot_general(a, b, (((1,), (1,)), ((), ())), preferred_element_type=F32)


def tn(a, b):
    return lax.dot_general(a, b, (((0,), (0,)), ((), ())), preferred_element_type=F32)


def aligned(value, step):
    return pl.multiple_of(value, step)


def stack_rows(rows):
    place = lax.broadcasted_iota(jnp.int32, (RANK, rows[0].shape[1]), 0)
    stacked = jnp.zeros(place.shape, F32)
    for n, row in enumerate(rows):
        stacked = jnp.where(place == n, row, stacked)
    return stacked.astype(BF16)


class Slots:
    def __init__(self):
        self.used = 0

    def take(self, count=1):
        first = self.used
        self.used += count
        return first


class Plan:
    def __init__(self, mesh, tokens, slice_width, head_width, hidden_width):
        self.groups = mesh.shape["dp"]
        self.rows = mesh.shape["row"]
        self.cols = mesh.shape["col"]
        assert self.rows == 4 and self.cols == 4 and self.groups % 2 == 0
        self.tokens = tokens
        self.half = tokens // 4
        self.pair = tokens // 2
        self.dl = slice_width
        self.width = slice_width * self.rows
        self.hl = head_width
        self.heads = head_width // HEAD_DIM
        self.fl = hidden_width
        self.images = self.groups * self.cols
        s, r = Slots(), Slots()
        self.s_x, self.r_x = s.take(4), r.take(4)
        self.s_c, self.r_c = s.take(4), r.take(4)
        self.s_cc, self.r_cc = s.take(), r.take()
        pieces = sum(PIECES)
        self.s_w, self.r_w = s.take(6 * pieces), r.take(16 * pieces)
        self.s_f, self.s_r = s.take(8 * pieces), s.take(8 * pieces)
        self.s_yx, self.r_yx = s.take(4), r.take(4)
        self.s_in, self.r_in = s.take(8), r.take(8)
        self.s_dp, self.r_dp = s.take(4), r.take(4)
        self.s_hp, self.r_hp = s.take(4), r.take(4)
        self.s_n1, self.r_n1 = s.take(2), r.take(2)
        self.s_n2, self.r_n2 = s.take(2), r.take(2)
        self.s_gb, self.r_gb = s.take(2), r.take(2)
        self.s_p, self.r_p = s.take(8), r.take(8)
        self.s_y, self.r_y = s.take(8), r.take(8)
        self.s_st, self.r_st = s.take(), r.take()
        self.s_o, self.r_o = s.take(4), r.take(4)
        self.s_low, self.r_low = s.take(16), r.take(16)
        self.s_gd, self.r_gd = s.take(2 * self.images), r.take(2 * self.images)
        self.s_gh, self.r_gh = s.take(2 * (self.groups + 2)), r.take(2 * (self.groups + 2))
        self.s_tr, self.r_tr = s.take(4), r.take(4)
        self.sends, self.receives = s.used, r.used

    def scratch(self):
        half, pair, width = self.half, self.pair, self.width
        tokens = lambda dt, w: VM((2, 2, half, w), dt)
        own = lambda dt, w: VM((2, half, w), dt)
        items = {
            "ss": pltpu.SemaphoreType.DMA((self.sends,)),
            "rs": pltpu.SemaphoreType.DMA((self.receives,)),
            "wq": VM((4, 3, self.dl, self.hl), BF16),
            "wo": VM((4, self.hl, self.dl), BF16),
            "w1": VM((4, self.dl, self.fl), BF16),
            "w2": VM((4, self.fl, self.dl), BF16),
            "tq": VM((3, self.dl, self.hl // 2), BF16),
            "to": VM((self.hl // 2, self.dl), BF16),
            "t1": VM((self.dl, self.fl // 2), BF16),
            "t2": VM((self.fl // 2, self.dl), BF16),
            "xg": own(BF16, width),
            "cg": tokens(BF16, width),
            "n1": tokens(BF16, width),
            "n2": tokens(BF16, width),
            "gb": tokens(BF16, width),
            "dpack": VM((7 * RANK, self.dl), BF16),
            "hpack": VM((5 * RANK, self.hl), BF16),
            "hwide": VM((3 * RANK, self.fl), BF16),
            "dfull": VM((4, 7 * RANK, self.dl), BF16),
            "ha": VM((5 * RANK, self.hl), BF16),
            "hb": VM((3 * RANK, self.fl), BF16),
            "m1": own(F32, 1),
            "i1": own(F32, 1),
            "m2": own(F32, 1),
            "i2": own(F32, 1),
            "qh": VM((self.heads, self.tokens, HEAD_DIM), BF16),
            "kh": VM((self.heads, self.tokens, HEAD_DIM), BF16),
            "vh": VM((self.heads, self.tokens, HEAD_DIM), BF16),
            "gh_h": VM((self.heads, self.tokens, HEAD_DIM), BF16),
            "ch": VM((self.heads, self.tokens, HEAD_DIM), BF16),
            "gqh": VM((self.heads, self.tokens, HEAD_DIM), BF16),
            "probs": VM((self.heads, self.tokens, self.tokens), BF16),
            "dk": VM((self.heads, HEAD_DIM, self.tokens), F32),
            "dv": VM((self.heads, HEAD_DIM, self.tokens), F32),
            "gqkv": VM((self.tokens, 3 * self.hl), BF16),
            "ctx": VM((2, pair, self.hl), BF16),
            "lowq": VM((2, pair, 3 * RANK), BF16),
            "low1": VM((2, pair, RANK), BF16),
            "glow2": VM((2, pair, RANK), BF16),
            "glowo": VM((2, pair, RANK), BF16),
            "act": VM((2, pair, self.fl), BF16),
            "slope": VM((2, pair, self.fl), F32),
            "gh": VM((2, pair, self.fl), BF16),
            "mixed": own(F32, width),
            "gmix": own(F32, width),
            "psum": VM((4, 2, 2, half, width), BF16),
            "prx": VM((4, 2, half, width), BF16),
            "ytx": VM((4, 2, half, width), BF16),
            "yrx": VM((2, 2, half, width), BF16),
            "yrh": VM((2, 2, half, width // 2), BF16),
            "stat": VM((384, 128), F32),
            "stx": VM((8, 384), F32),
            "sty": VM((8, 384), F32),
            "osend": VM((2, 2, half, self.dl), BF16),
            "ofull": VM((2, 2, 2, half, self.dl), BF16),
            "lowt": VM((4, 4, 3 * RANK, self.tokens), BF16),
            "gde": VM((3 * RANK, self.dl), BF16),
            "gdl": VM((4 * RANK, self.dl), BF16),
            "ghe": VM((2 * RANK, self.fl), BF16),
            "ghl": VM((4 * RANK, self.hl), BF16),
            "tre": VM((2 * RANK, self.fl), BF16),
            "trl": VM((4 * RANK, self.hl), BF16),
        }
        return items


INPUTS = (
    "labels", "mask", "x_in", "c_in", "wq_in", "wo_in", "w1_in", "w2_in", "g1_in", "b1_in", "ob_in", "g2_in", "b2_in", "sb_in", "qb_in", "fb_in",
    "qd_in", "qu_in", "od_in", "ou_in", "fd_in", "fu_in", "sd_in", "su_in",
)
OUTPUTS = ("o_out", "g_out", "gde_all", "gdl_all", "ghe_all", "ghl_all")


def block_kernel(plan, names, *refs):
    g = dict(zip(INPUTS + OUTPUTS + names, refs))
    r_ = type("Refs", (), g)
    ss, rs = r_.ss, r_.rs
    half, pair, width, dl, hl, fl = plan.half, plan.pair, plan.width, plan.dl, plan.hl, plan.fl
    mid = width // 2
    x = lax.axis_index("dp")
    r = lax.axis_index("row")
    z = lax.axis_index("col")
    y = lax.div(r, 2)
    k = lax.rem(r, 2)
    hx = lax.rem(x, 2)
    twin_x = (x + 1 - 2 * hx, r, z)
    twin_y = (x, 2 * (1 - y) + k, z)
    twin_k = (x, 2 * y + 1 - k, z)
    kd, e_own = lax.div(z, 2), lax.rem(z, 2)

    def rc(src, dst, send, recv, device):
        return pltpu.make_async_remote_copy(
            src_ref=src, dst_ref=dst, send_sem=ss.at[send], recv_sem=rs.at[recv],
            device_id=device, device_id_type=MESH,
        )

    def wait_recv(dst, recv):
        rc(dst, dst, 0, recv, twin_k).wait_recv()

    def wait_send(src, send):
        rc(src, src, send, 0, twin_k).wait_send()

    barrier = pltpu.get_barrier_semaphore()
    total = plan.groups * 16
    place = (x * 4 + r) * 4 + z

    def greet(o, _):
        t = lax.rem(place + o, total)
        pl.semaphore_signal(
            barrier, inc=1, device_id=(lax.div(t, 16), lax.rem(lax.div(t, 4), 4), lax.rem(t, 4)),
            device_id_type=MESH,
        )
        return 0

    lax.fori_loop(1, total, greet, 0)
    pl.semaphore_wait(barrier, total - 1)

    my_cols = pl.ds(aligned(r * dl, dl), dl)
    group = (
        (1, twin_y, k),
        (2, (x, 2 * (1 - y) + 1 - k, z), 1 - k),
        (3, twin_k, 1 - k),
    )

    def send_tokens(src, dst_of, first_s, first_r):
        for o, device, core in group:
            rc(src.at[:, core], dst_of(core), first_s + o, first_r + r, device).start()
        pltpu.make_async_copy(src.at[:, k], dst_of(k), ss.at[first_s]).start()

    def wait_tokens(src, dst_of, first_s, first_r):
        pltpu.make_async_copy(src.at[:, k], dst_of(k), ss.at[first_s]).wait()
        for o in range(1, 4):
            wait_recv(dst_of(k), first_r + lax.rem(r + o, 4))

    x_dst = lambda core: r_.xg.at[:, :, my_cols]
    c_dst = lambda core: r_.cg.at[:, core, :, my_cols]

    w_in = (r_.wq_in, r_.wo_in, r_.w1_in, r_.w2_in)
    w_at = (r_.tq, r_.to, r_.t1, r_.t2)
    w_to = (r_.wq, r_.wo, r_.w1, r_.w2)
    r_other = 2 * (1 - y) + k
    keeps = kd == k

    def span(start, size):
        return pl.ds(aligned(start, size), size)

    def cut(ref, t, first, lead=(), m=None, h=None):
        if t == 0:
            rows = slice(None) if h is None else span(h * (dl // 2), dl // 2)
            return ref.at[lead + (slice(None), rows, span(first * (hl // 2), hl // 2))]
        if t == 2:
            rows = slice(None) if h is None else span((2 * h + m) * (dl // 4), dl // 4)
            return ref.at[lead + (rows, span(first * (fl // 2), fl // 2))]
        size = (hl if t == 1 else fl) // 2
        if h is None:
            return ref.at[lead + (span(first * size, size), slice(None))]
        step = size // (2 * PIECES[t])
        return ref.at[lead + (span(first * size + (2 * m + h) * step, step), slice(None))]

    def piece(t, m):
        return sum(PIECES[:t]) + m

    def source(t, which, m=None, h=None):
        return cut(w_at[t], t, 0, (), m, h) if which else cut(w_in[t], t, y, (), m, h)

    def slot(t, s, e, m=None, h=None):
        return cut(w_to[t], t, e, (s,), m, h)

    def turn_weights(t):
        return rc(cut(w_in[t], t, 1 - y), w_at[t], plan.s_yx + t, plan.r_yx + t, twin_y)

    targets = (3 - z, lax.rem(2 + 3 * z, 5), 1 + lax.div(z, 3))
    three = lax.rem(z, 3) == 0

    def push_copy(t, m, which, i):
        n, s = piece(t, m), (r, r_other)[which]
        return rc(
            source(t, which, m, hx), slot(t, s, e_own, m, hx), plan.s_w + n * 6 + which * 3 + i,
            plan.r_w + n * 16 + s * 4 + e_own * 2 + hx, (x, 2 * y + kd, targets[i]),
        )

    def own_weights(t, which):
        s = (r, r_other)[which]
        return pltpu.make_async_copy(
            source(t, which), slot(t, s, e_own), ss.at[plan.s_in + t * 2 + which]
        )

    def near_copy(t, which, s):
        place = t * 2 + which
        return rc(source(t, which), slot(t, s, e_own), plan.s_in + place, plan.r_in + place, twin_k)

    def push_weights(t, which):
        if which:
            turn_weights(t).wait_recv()
        for m in range(PIECES[t]):
            push_copy(t, m, which, 0).start()
            push_copy(t, m, which, 1).start()
            pl.when(three)(lambda: push_copy(t, m, which, 2).start())
        pl.when(keeps)(lambda: own_weights(t, which).start())
        near = near_copy(t, which, (r, r_other)[which])
        pl.when(jnp.logical_not(keeps))(lambda: near.start())

    def arrived(t, m, s, e, h):
        n = piece(t, m)
        wait_recv(slot(t, s, e, m, h), plan.r_w + n * 16 + s * 4 + e * 2 + h)

    def pass_copy(t, m, s, e, base, device):
        n, part = piece(t, m), slot(t, s, e, m, hx)
        return rc(
            part, part, base + n * 8 + s * 2 + e, plan.r_w + n * 16 + s * 4 + e * 2 + hx, device
        )

    def over_x(t, m, s, e):
        return pass_copy(t, m, s, e, plan.s_f, twin_x)

    def over_z(t, m, s, e):
        return pass_copy(t, m, s, e, plan.s_r, (x, r, 3 * lax.rem(z + 1, 2)))

    def passes_on(e):
        return 2 * k + e + z == 3

    def foreign(e):
        return 2 * k + e != z

    middle = lax.rem(z + 1, 4) >= 2

    def forward_weights(t, m, which, part):
        e = lax.rem(z + 1 + part, 2)
        lane = 2 * (y, 1 - y)[which]

        @pl.when(foreign(e))
        def _():
            for core in range(2):
                s = lane + core
                arrived(t, m, s, e, hx)

                @pl.when(jnp.logical_and(middle, passes_on(e)))
                def _():
                    over_z(t, m, s, e).start()

                over_x(t, m, s, e).start()

    pending = [
        (t, m, which, part)
        for t in (2, 3) for which in range(2) for m in range(PIECES[t]) for part in range(2)
    ]

    def serve(count=1):
        for _ in range(min(count, len(pending))):
            forward_weights(*pending.pop(0))

    def wait_piece(t, m, e):
        @pl.when(foreign(e))
        def _():
            for s in range(4):
                arrived(t, m, s, e, 1 - hx)

        if m > 0:
            return

        @pl.when(jnp.logical_not(foreign(e)))
        def _():
            for which in range(2):
                own_weights(t, which).wait()
                near_copy(t, which, (2 * y + 1 - k, 2 * (1 - y) + 1 - k)[which]).wait_recv()

    def wait_weights(t):
        for m in range(PIECES[t]):
            for e in range(2):
                wait_piece(t, m, e)

    def finish_weights(t):
        turn_weights(t).wait_send()
        for which in range(2):
            for m in range(PIECES[t]):
                push_copy(t, m, which, 0).wait_send()
                push_copy(t, m, which, 1).wait_send()
                pl.when(three)(lambda: push_copy(t, m, which, 2).wait_send())
            near = near_copy(t, which, r)
            pl.when(jnp.logical_not(keeps))(lambda: near.wait_send())
        for m in range(PIECES[t]):
            for e in range(2):
                @pl.when(foreign(e))
                def _():
                    for s in range(4):
                        @pl.when(jnp.logical_and(middle, passes_on(e)))
                        def _():
                            over_z(t, m, s, e).wait_send()

                        over_x(t, m, s, e).wait_send()

    turn_weights(0).start()
    push_weights(0, 0)
    turn_weights(1).start()
    send_tokens(r_.x_in, x_dst, plan.s_x, plan.r_x)
    turn_weights(2).start()
    turn_weights(3).start()

    mine = r_.labels[z]
    theirs = r_.labels[r]
    for p in range(3):
        r_.dpack[p * RANK : (p + 1) * RANK] = r_.qd_in[p, mine]
        r_.hpack[p * RANK : (p + 1) * RANK] = r_.qu_in[p, theirs]
    r_.dpack[3 * RANK : 4 * RANK] = r_.ou_in[mine]
    r_.dpack[4 * RANK : 5 * RANK] = r_.fd_in[mine]
    r_.dpack[5 * RANK : 6 * RANK] = r_.su_in[mine]
    vectors = (r_.g1_in, r_.b1_in, r_.ob_in, r_.g2_in, r_.b2_in, r_.sb_in)
    r_.dpack[6 * RANK : 7 * RANK] = stack_rows([v[...].astype(F32).reshape(1, dl) for v in vectors])
    r_.hpack[3 * RANK : 4 * RANK] = r_.od_in[theirs]
    qkv_bias = r_.qb_in[...].astype(F32)
    fc1_bias = r_.fb_in[...].astype(F32).reshape(1, fl)
    r_.hpack[4 * RANK : 5 * RANK] = stack_rows([qkv_bias[0:1], qkv_bias[1:2]])
    r_.hwide[2 * RANK : 3 * RANK] = stack_rows([fc1_bias])
    r_.hwide[0:RANK] = r_.fu_in[theirs]
    r_.hwide[RANK : 2 * RANK] = r_.sd_in[theirs]

    def dpack_copy(o):
        return rc(
            r_.dpack, r_.dfull.at[r], plan.s_dp + o, plan.r_dp + r, (x, lax.rem(r + o, 4), z)
        )

    for o in (1, 2, 3):
        dpack_copy(o).start()
    r_.dfull[r] = r_.dpack[...]
    h_parts_in = ((r_.hpack, r_.ha, hl // 2), (r_.hwide, r_.hb, fl // 2))

    def hpack_each(b, remote, own=None):
        away = jnp.logical_or(r != z, 2 * b + kd != r)
        for n, (src, dst, size) in enumerate(h_parts_in):
            piece_in, piece_to = src.at[:, span(b * size, size)], dst.at[:, span(e_own * size, size)]
            copy = rc(
                piece_in, piece_to, plan.s_hp + b * 2 + n, plan.r_hp + e_own * 2 + n,
                (x, 2 * b + kd, r),
            )
            pl.when(away)(functools.partial(remote, copy))
            if own is not None:
                same = pltpu.make_async_copy(piece_in, piece_to, ss.at[plan.s_hp + b * 2 + n])
                pl.when(jnp.logical_not(away))(functools.partial(own, same))

    def begin(copy):
        copy.start()

    def sent(copy):
        copy.wait_send()

    def done(copy):
        copy.wait()

    for b in range(2):
        hpack_each(b, begin, begin)

    def wait_hpack():
        for b in range(2):
            hpack_each(b, lambda copy: None, done)
        for e in range(2):
            @pl.when(jnp.logical_or(r != z, foreign(e)))
            def _():
                for n, (_, dst, size) in enumerate(h_parts_in):
                    wait_recv(dst.at[:, span(e * size, size)], plan.r_hp + e * 2 + n)

    def d_rows(first, count):
        return jnp.concatenate([r_.dfull[s, first : first + count, :] for s in range(4)], axis=1)

    def d_vector(index):
        rows = [r_.dfull[s, 6 * RANK : 7 * RANK, :].astype(F32) for s in range(4)]
        return jnp.concatenate([row[index : index + 1] for row in rows], axis=1)

    def h_vector(index):
        return r_.ha[4 * RANK : 5 * RANK, :].astype(F32)[index : index + 1]

    def fc1_vector(cols):
        return r_.hb[2 * RANK : 3 * RANK, cols].astype(F32)[0:1]

    def steps(body):
        def run(i, _):
            body(pl.ds(aligned(i * STEP, STEP), STEP))
            return 0

        lax.fori_loop(0, half // STEP, run, 0)

    def twin_send(ref, i, first_s, first_r):
        rc(ref.at[i, k], ref.at[i, k], first_s + i, first_r + i, twin_k).start()

    def twin_wait(ref, i, first_r):
        wait_recv(ref.at[i, 1 - k], first_r + i)

    def norm(values, gain, bias):
        center = jnp.sum(values, axis=-1, keepdims=True) * (1.0 / width)
        spread = jnp.sum(values * values, axis=-1, keepdims=True) * (1.0 / width) - center * center
        scaling = lax.rsqrt(spread + EPSILON)
        return (values - center) * scaling * gain + bias, center, scaling

    push_weights(0, 1)
    push_weights(1, 0)
    forward_weights(0, 0, 0, 0)
    forward_weights(0, 0, 0, 1)
    push_weights(1, 1)
    push_weights(2, 0)
    forward_weights(0, 0, 1, 0)
    forward_weights(0, 0, 1, 1)
    for o in (1, 2, 3):
        wait_recv(r_.dfull.at[r], plan.r_dp + lax.rem(r + o, 4))
    wait_tokens(r_.x_in, x_dst, plan.s_x, plan.r_x)
    gain_one, bias_one = d_vector(0), d_vector(1)
    for i in range(2):

        def first_norm(rows, i=i):
            normed, center, scaling = norm(r_.xg[i, rows].astype(F32), gain_one, bias_one)
            r_.n1[i, k, rows] = normed.astype(BF16)
            r_.m1[i, rows] = center
            r_.i1[i, rows] = scaling

        steps(first_norm)
        twin_send(r_.n1, i, plan.s_n1, plan.r_n1)

    forward_weights(1, 0, 0, 0)
    forward_weights(1, 0, 0, 1)
    push_weights(2, 1)
    push_weights(3, 0)
    forward_weights(1, 0, 1, 0)
    forward_weights(1, 0, 1, 1)
    wait_hpack()
    for i in range(2):
        twin_wait(r_.n1, i, plan.r_n1)
    wait_weights(0)

    row_block = lax.broadcasted_iota(jnp.int32, (3 * RANK, hl), 0) // RANK
    up_rows = r_.ha[0 : 3 * RANK, :]
    ups = [jnp.where(row_block == p, up_rows, jnp.zeros_like(up_rows)) for p in range(3)]
    q_bias = (h_vector(0), None, h_vector(1))

    def project_qkv(i):
        tokens = r_.n1[i].reshape(pair, width)
        low = nt(tokens, d_rows(0, 3 * RANK)).astype(BF16)
        r_.lowq[i] = low
        for p, out in enumerate((r_.qh, r_.kh, r_.vh)):
            value = nn(tokens, r_.wq[:, p].reshape(width, hl)) + nn(low, ups[p])
            if q_bias[p] is not None:
                value = value + q_bias[p]
            value = value.astype(BF16)
            if p == 0:
                value = value * jnp.asarray(HEAD_DIM ** (-0.5), BF16)
            for h in range(plan.heads):
                out[h, i * pair : (i + 1) * pair, :] = value[:, h * HEAD_DIM : (h + 1) * HEAD_DIM]

    project_qkv(0)
    serve(2)
    project_qkv(1)
    push_weights(3, 1)
    serve()
    send_tokens(r_.c_in, c_dst, plan.s_c, plan.r_c)

    mask_rows = r_.mask[...]
    picked = lax.broadcasted_iota(jnp.int32, mask_rows.shape, 0) == z
    valid = jnp.sum(jnp.where(picked, mask_rows, 0), axis=0, keepdims=True)
    shift = jnp.where(valid > 0, 0.0, MASKED_SCORE).astype(F32)

    def attend(i, first, last):
        def one(t, _):
            h, u = lax.div(t, 2), lax.rem(t, 2)
            rows = pl.ds(aligned(i * pair + u * half, half), half)
            scores = nt(r_.qh[h, rows, :], r_.kh[h]) + shift
            powered = jnp.exp(scores - jnp.max(scores, axis=-1, keepdims=True))
            summed = jnp.sum(powered, axis=-1, keepdims=True)
            probs = (powered * (1.0 / summed)).astype(BF16)
            r_.probs[h, rows, :] = probs
            r_.ch[h, rows, :] = nn(probs, r_.vh[h]).astype(BF16)
            return 0

        lax.fori_loop(2 * first, 2 * last, one, 0)
        if last < plan.heads:
            return
        r_.ctx[i] = jnp.concatenate(
            [r_.ch[h, i * pair : (i + 1) * pair, :] for h in range(plan.heads)], axis=1
        )

    def keep_sum(which, i, s, value):
        r_.psum[which, i, :, :, s * dl : (s + 1) * dl] = value.reshape(2, half, dl).astype(BF16)

    def core_copy(which, i):
        slot = plan.s_p + which * 2 + i, plan.r_p + which * 2 + i
        return rc(r_.psum.at[which, i, 1 - k], r_.prx.at[which, i], slot[0], slot[1], twin_k)

    def chip_sum(which, i, also=None):
        core_copy(which, i).wait_recv()

        def add(rows):
            both = r_.psum[which, i, k, rows].astype(F32) + r_.prx[which, i, rows].astype(F32)
            r_.ytx[which, i, rows] = both.astype(BF16)
            if also is not None:
                also(rows, both)

        steps(add)
        if also is None or i == 0:
            y_copy(which, i).start()

    other_half = pl.ds(aligned((1 - y) * mid, mid), mid)
    own_half = pl.ds(aligned(y * mid, mid), mid)

    def y_copy(which, i):
        slot = plan.s_y + which * 2 + i, plan.r_y + which * 2 + i
        if which < 2:
            return rc(r_.ytx.at[which, i], r_.yrx.at[which, i], slot[0], slot[1], twin_y)
        src = r_.ytx.at[which, i, :, other_half]
        return rc(src, r_.yrh.at[which - 2, i], slot[0], slot[1], twin_y)

    def project_out(i):
        low = nt(r_.ctx[i], r_.ha[3 * RANK : 4 * RANK, :]).astype(BF16)
        for s in range(4):
            keep_sum(0, i, s, nn(r_.ctx[i], r_.wo[s]) + nn(low, r_.dfull[s, 3 * RANK : 4 * RANK, :]))
        core_copy(0, i).start()

    middle_head = plan.heads // 2
    attend(0, 0, middle_head)
    serve()
    attend(0, middle_head, plan.heads)
    wait_weights(1)
    project_out(0)
    serve()
    attend(1, 0, middle_head)
    chip_sum(0, 0)
    serve()
    attend(1, middle_head, plan.heads)
    project_out(1)
    serve()
    chip_sum(0, 1)
    wait_tokens(r_.c_in, c_dst, plan.s_c, plan.r_c)
    c_relay = rc(r_.cg.at[:, k], r_.cg.at[:, k], plan.s_cc, plan.r_cc, twin_k)
    c_relay.start()
    serve(4)

    out_bias, gain_two, bias_two, fc2_bias = (d_vector(n) for n in (2, 3, 4, 5))

    def second_norm(i):
        y_copy(0, i).wait_recv()

        def one(rows):
            branch = r_.ytx[0, i, rows].astype(F32) + r_.yrx[0, i, rows].astype(F32)
            mixed = r_.xg[i, rows].astype(F32) + branch + out_bias
            normed, center, scaling = norm(mixed, gain_two, bias_two)
            r_.mixed[i, rows] = mixed
            r_.n2[i, k, rows] = normed.astype(BF16)
            r_.m2[i, rows] = center
            r_.i2[i, rows] = scaling

        steps(one)
        twin_send(r_.n2, i, plan.s_n2, plan.r_n2)


    def hidden_units(i):
        twin_wait(r_.n2, i, plan.r_n2)
        tokens = r_.n2[i].reshape(pair, width)
        low = nt(tokens, d_rows(4 * RANK, RANK)).astype(BF16)
        r_.low1[i] = low
        for f in range(fl // 256):
            cols = slice(f * 256, (f + 1) * 256)
            hidden = nn(tokens, r_.w1[:, :, cols].reshape(width, 256))
            hidden = hidden + nn(low, r_.hb[0:RANK, cols]) + fc1_vector(cols)
            lower = 0.5 * (1.0 + lax.erf(hidden * SQRT_HALF))
            r_.act[i, :, cols] = (hidden * lower).astype(BF16)
            r_.slope[i, :, cols] = lower + hidden * jnp.exp(-0.5 * hidden * hidden) * INV_ROOT_TAU

    second_norm(0)
    wait_weights(2)
    hidden_units(0)
    serve(2)
    second_norm(1)
    serve()
    hidden_units(1)
    wait_recv(r_.cg.at[:, 1 - k], plan.r_cc)

    def low_grads(i):
        tokens = r_.cg[i].reshape(pair, width)
        r_.glow2[i] = nt(tokens, d_rows(5 * RANK, RANK)).astype(BF16)

    def hidden_grads(f, i):
        cols = slice(f * fl // 4, (f + 1) * fl // 4)
        weight = jnp.concatenate([r_.w2[s, cols, :] for s in range(4)], axis=1)
        grad = nt(r_.cg[i].reshape(pair, width), weight)
        grad = grad + nn(r_.glow2[i], r_.hb[RANK : 2 * RANK, cols])
        r_.gh[i, :, cols] = (grad * r_.slope[i, :, cols]).astype(BF16)

    def hidden_back(i):
        low = nt(r_.gh[i], r_.hb[0:RANK, :]).astype(BF16)
        for s in range(4):
            value = nt(r_.gh[i], r_.w1[s]) + nn(low, r_.dfull[s, 4 * RANK : 5 * RANK, :])
            keep_sum(1, i, s, value)
        core_copy(1, i).start()

    def second_layer(i):
        low = nt(r_.act[i], r_.hb[RANK : 2 * RANK, :]).astype(BF16)
        for s in range(4):
            value = nn(r_.act[i], r_.w2[s]) + nn(low, r_.dfull[s, 5 * RANK : 6 * RANK, :])
            keep_sum(2, i, s, value)
        core_copy(2, i).start()

    def low_copy(n, o):
        count = 3 * RANK if n == 3 else RANK
        own = r_.lowt.at[n, r, 0:count]
        slot = plan.s_low + n * 4 + o, plan.r_low + n * 4 + r
        return rc(own, own, slot[0], slot[1], (x, lax.rem(r + o, 4), z))

    def share_low(n, value):
        r_.lowt[n, r, 0 : value.shape[0]] = value.astype(BF16)
        for o in (1, 2, 3):
            low_copy(n, o).start()

    def total_low(n):
        count = 3 * RANK if n == 3 else RANK
        for o in (1, 2, 3):
            wait_recv(r_.lowt.at[n, r, 0:count], plan.r_low + n * 4 + lax.rem(r + o, 4))
        parts = [r_.lowt[n, s, 0:count].astype(F32) for s in range(4)]
        return ((parts[0] + parts[1]) + (parts[2] + parts[3])).astype(BF16)

    def all_rows(ref):
        return ref[...].reshape(2 * pair, ref.shape[-1])

    def own_copy(src, dst, slot):
        return pltpu.make_async_copy(src, dst, ss.at[slot])

    def over(count, body):
        def run(o, _):
            body(o)
            return 0

        lax.fori_loop(1, count, run, 0)

    d_parts = ((r_.gde, r_.gde_all), (r_.gdl, r_.gdl_all))
    h_parts = ((r_.ghe, r_.tre, r_.ghe_all), (r_.ghl, r_.trl, r_.ghl_all))

    def d_copy(n, o):
        src, dst = d_parts[n]
        t = lax.rem(x * 4 + z + o, plan.images)
        base = n * plan.images
        return rc(
            src, dst.at[x, z], plan.s_gd + base + o, plan.r_gd + base + x * 4 + z,
            (lax.div(t, 4), r, lax.rem(t, 4)),
        )

    h_places = plan.groups + 2

    def h_across_y(n):
        _, src, dst = h_parts[n]
        base = n * h_places
        return rc(src, dst.at[x, y, k], plan.s_gh + base, plan.r_gh + base, twin_y)

    def h_across_x(n, o):
        block = h_parts[n][2].at[x, :, k]
        base = n * h_places + o
        device = (lax.rem(x + o, plan.groups), r, z)
        return rc(block, block, plan.s_gh + base, plan.r_gh + base, device)

    def h_across_k(n):
        block = h_parts[n][2].at[:, :, k]
        base = n * h_places + plan.groups
        return rc(block, block, plan.s_gh + base, plan.r_gh + base, twin_k)

    def h_own(n):
        _, src, dst = h_parts[n]
        return own_copy(src, dst.at[x, y, k], plan.s_gh + n * h_places + plan.groups + 1)

    def turn_each(n, e, remote, own=None):
        src, dst, _ = h_parts[n]
        size = src.shape[1] // 2
        piece_in, piece_to = src.at[:, span(e * size, size)], dst.at[:, span(y * size, size)]
        away = jnp.logical_or(r != z, foreign(e))
        copy = rc(
            piece_in, piece_to, plan.s_tr + n * 2 + e, plan.r_tr + n * 2 + y, (x, z, 2 * k + e)
        )
        pl.when(away)(functools.partial(remote, copy))
        if own is not None:
            same = pltpu.make_async_copy(piece_in, piece_to, ss.at[plan.s_tr + n * 2 + e])
            pl.when(jnp.logical_not(away))(functools.partial(own, same))

    def start_d(n):
        src, dst = d_parts[n]
        own_copy(src, dst.at[x, z], plan.s_gd + n * plan.images).start()
        over(plan.images, lambda o: d_copy(n, o).start())

    def turn_h(n):
        for e in range(2):
            turn_each(n, e, begin, begin)

    def start_h(n):
        _, src, _ = h_parts[n]
        size = src.shape[1] // 2
        for e in range(2):
            turn_each(n, e, lambda copy: None, done)
        for b in range(2):
            @pl.when(jnp.logical_or(r != z, 2 * b + kd != r))
            def _():
                wait_recv(src.at[:, span(b * size, size)], plan.r_tr + n * 2 + b)
        h_own(n).start()
        h_across_y(n).start()

    def spread_h(n):
        h_own(n).wait()
        wait_recv(h_parts[n][2].at[x, 1 - y, k], plan.r_gh + n * h_places)
        over(plan.groups, lambda o: h_across_x(n, o).start())

    def share_h(n):
        def one(o):
            other = lax.rem(x + plan.groups - o, plan.groups)
            wait_recv(h_parts[n][2].at[other, :, k], plan.r_gh + n * h_places + o)

        over(plan.groups, one)
        h_across_k(n).start()

    def finish_d(n):
        src, dst = d_parts[n]
        base = n * plan.images
        own_copy(src, dst.at[x, z], plan.s_gd + base).wait()

        def one(o):
            d_copy(n, o).wait_send()
            t = lax.rem(x * 4 + z + o, plan.images)
            wait_recv(dst.at[lax.div(t, 4), lax.rem(t, 4)], plan.r_gd + base + t)

        over(plan.images, one)

    def finish_h(n):
        for e in range(2):
            turn_each(n, e, sent)
        h_across_y(n).wait_send()
        over(plan.groups, lambda o: h_across_x(n, o).wait_send())
        h_across_k(n).wait_send()
        wait_recv(h_parts[n][2].at[:, :, 1 - k], plan.r_gh + n * h_places + plan.groups)

    def my_slice(ref):
        return ref[:, :, :, my_cols].reshape(2 * pair, dl)

    low_grads(0)
    low_grads(1)
    serve(16)
    for m, e in ((0, 0), (0, 1), (1, 0), (1, 1)):
        f = 2 * e + m
        wait_piece(3, m, e)
        hidden_grads(f, 0)
        if f == 3:
            hidden_back(0)
        hidden_grads(f, 1)
    chip_sum(1, 0)
    hidden_back(1)
    chip_sum(1, 1)
    second_layer(0)
    second_layer(1)
    share_low(2, nt(r_.hb[0:RANK, :], all_rows(r_.gh)))
    share_low(0, nt(r_.ha[3 * RANK : 4 * RANK, :], all_rows(r_.ctx)))
    share_low(1, nt(r_.hb[RANK : 2 * RANK, :], all_rows(r_.act)))
    chip_sum(2, 0)
    chip_sum(2, 1)

    def norm_grad(incoming, normal, scaling, gain):
        scaled = incoming * gain
        first = jnp.sum(scaled, axis=-1, keepdims=True) * (1.0 / width)
        second = jnp.sum(scaled * normal, axis=-1, keepdims=True) * (1.0 / width)
        return scaling * (scaled - first - normal * second)

    def mixed_grad(i):
        y_copy(1, i).wait_recv()

        def one(rows):
            incoming = r_.ytx[1, i, rows].astype(F32) + r_.yrx[1, i, rows].astype(F32)
            scaling = r_.i2[i, rows]
            normal = (r_.mixed[i, rows] - r_.m2[i, rows]) * scaling
            grad = r_.cg[i, k, rows].astype(F32) + norm_grad(incoming, normal, scaling, gain_two)
            r_.gmix[i, rows] = grad
            r_.gb[i, k, rows] = grad.astype(BF16)

        steps(one)
        twin_send(r_.gb, i, plan.s_gb, plan.r_gb)

    r_.dk[...] = jnp.zeros_like(r_.dk)
    r_.dv[...] = jnp.zeros_like(r_.dv)

    def attend_back(i):
        twin_wait(r_.gb, i, plan.r_gb)
        tokens = r_.gb[i].reshape(pair, width)
        low = nt(tokens, d_rows(3 * RANK, RANK)).astype(BF16)
        r_.glowo[i] = low
        weight = jnp.concatenate([r_.wo[s] for s in range(4)], axis=1)
        value = (nt(tokens, weight) + nn(low, r_.ha[3 * RANK : 4 * RANK, :])).astype(BF16)
        for h in range(plan.heads):
            r_.gh_h[h, i * pair : (i + 1) * pair, :] = value[:, h * HEAD_DIM : (h + 1) * HEAD_DIM]

        def one(t, _):
            h, u = lax.div(t, 2), lax.rem(t, 2)
            rows = pl.ds(aligned(i * pair + u * half, half), half)
            grad, probs = r_.gh_h[h, rows, :], r_.probs[h, rows, :]
            inner = jnp.sum(
                grad.astype(F32) * r_.ch[h, rows, :].astype(F32), axis=-1, keepdims=True
            )
            scores = (probs.astype(F32) * (nt(grad, r_.vh[h]) - inner)).astype(BF16)
            r_.gqh[h, rows, :] = (nn(scores, r_.kh[h]) * HEAD_DIM ** (-0.5)).astype(BF16)
            r_.dk[h] += tn(r_.qh[h, rows, :], scores)
            r_.dv[h] += tn(grad, probs)
            return 0

        lax.fori_loop(0, 2 * plan.heads, one, 0)

    mixed_grad(0)
    r_.ghe[0:RANK] = tn(all_rows(r_.low1), all_rows(r_.gh)).astype(BF16)
    r_.ghe[RANK : 2 * RANK] = tn(all_rows(r_.glow2), all_rows(r_.act)).astype(BF16)
    turn_h(0)
    attend_back(0)
    start_h(0)
    mixed_grad(1)
    r_.gde[0:RANK] = nn(total_low(2), my_slice(r_.n2)).astype(BF16)
    r_.gde[RANK : 2 * RANK] = nn(total_low(1), my_slice(r_.cg)).astype(BF16)
    r_.gde[2 * RANK : 3 * RANK] = jnp.zeros((RANK, dl), BF16) + mine.astype(F32).astype(BF16)
    start_d(0)
    spread_h(0)
    attend_back(1)
    share_h(0)
    r_.gqkv[:, 0:hl] = jnp.concatenate([r_.gqh[h] for h in range(plan.heads)], axis=1)
    r_.gqkv[:, hl : 2 * hl] = r_.dk[...].reshape(hl, plan.tokens).T.astype(BF16)
    r_.gqkv[:, 2 * hl : 3 * hl] = r_.dv[...].reshape(hl, plan.tokens).T.astype(BF16)
    up_block = jnp.concatenate(ups, axis=1)

    def project_back(i):
        rows = slice(i * pair, (i + 1) * pair)
        grads = r_.gqkv[rows, :]
        low = nt(grads, up_block).astype(BF16)
        for s in range(4):
            weight = jnp.concatenate([r_.wq[s, p] for p in range(3)], axis=1)
            keep_sum(3, i, s, nt(grads, weight) + nn(low, r_.dfull[s, 0 : 3 * RANK, :]))
        core_copy(3, i).start()

    project_back(0)
    share_low(3, nt(up_block, r_.gqkv[...]))
    project_back(1)
    lane = lax.broadcasted_iota(jnp.int32, (STEP, 128), 1)
    r_.stat[...] = jnp.zeros_like(r_.stat)

    def input_sums(i):
        def one(rows, incoming):
            normal = (r_.xg[i, rows].astype(F32) - r_.m1[i, rows]) * r_.i1[i, rows]
            scaled = incoming * gain_one
            first = jnp.sum(scaled, axis=-1, keepdims=True)
            second = jnp.sum(scaled * normal, axis=-1, keepdims=True)
            both = jnp.where(lane == 0, first, jnp.where(lane == 1, second, 0.0))
            r_.stat[pl.ds(aligned(i * half + rows.start, STEP), STEP)] = both

        return one

    chip_sum(3, 0, input_sums(0))
    chip_sum(3, 1, input_sums(1))
    r_.stx[...] = r_.stat[...].T[0:8]
    stat_copy = rc(r_.stx, r_.sty, plan.s_st, plan.r_st, twin_y)
    stat_copy.start()
    y_copy(3, 1).start()
    up_grad = jnp.zeros((3 * RANK, hl), F32)
    for p in range(3):
        product = tn(all_rows(r_.lowq), r_.gqkv[:, p * hl : (p + 1) * hl])
        up_grad = up_grad + jnp.where(row_block == p, product, 0.0)
    r_.ghl[0 : 3 * RANK] = up_grad.astype(BF16)
    r_.ghl[3 * RANK : 4 * RANK] = tn(all_rows(r_.glowo), all_rows(r_.ctx)).astype(BF16)
    turn_h(1)
    r_.gdl[3 * RANK : 4 * RANK] = nn(total_low(0), my_slice(r_.gb)).astype(BF16)
    r_.gdl[0 : 3 * RANK] = nn(total_low(3), my_slice(r_.n1)).astype(BF16)
    start_d(1)
    start_h(1)

    def out_copy(n, i):
        slot = plan.s_o + n * 2 + i, plan.r_o + n * 2 + i
        return rc(r_.osend.at[n, i], r_.ofull.at[n, i, k], slot[0], slot[1], twin_k)

    def place_out(n, i, rows, value):
        left, right = value[:, 0:dl].astype(BF16), value[:, dl : 2 * dl].astype(BF16)
        first = k == 0
        r_.ofull[n, i, k, rows] = jnp.where(first, left, right)
        r_.osend[n, i, rows] = jnp.where(first, right, left)

    def half_vector(vector):
        return jnp.where(y == 0, vector[:, 0:mid], vector[:, mid:width])

    bias_half = half_vector(fc2_bias)
    for i in range(2):
        if i == 1:
            spread_h(1)
        y_copy(2, i).wait_recv()

        def last_sum(rows, i=i):
            value = r_.ytx[2, i, rows, own_half].astype(F32) + r_.yrh[0, i, rows].astype(F32)
            place_out(0, i, rows, r_.mixed[i, rows, own_half] + value + bias_half)

        steps(last_sum)
        out_copy(0, i).start()

    gain_half = half_vector(gain_one)
    share_h(1)
    stat_copy.wait_recv()
    joined = r_.stx[...] + r_.sty[...]
    r_.stat[...] = jnp.concatenate([joined, jnp.zeros((120, 384), F32)], axis=0).T
    for i in range(2):
        y_copy(3, i).wait_recv()

        def last_grad(t, _, i=i):
            rows = pl.ds(aligned(t * STEP, STEP), STEP)
            stats = r_.stat[pl.ds(aligned(i * half + t * STEP, STEP), STEP)] * (1.0 / width)
            incoming = r_.ytx[3, i, rows, own_half].astype(F32) + r_.yrh[1, i, rows].astype(F32)
            scaling = r_.i1[i, rows]
            normal = (r_.xg[i, rows, own_half].astype(F32) - r_.m1[i, rows]) * scaling
            grad = scaling * (incoming * gain_half - stats[:, 0:1] - normal * stats[:, 1:2])
            place_out(1, i, rows, r_.gmix[i, rows, own_half] + grad)
            return 0

        lax.fori_loop(0, half // STEP, last_grad, 0)
        out_copy(1, i).start()

    for n in range(2):
        for i in range(2):
            wait_recv(r_.ofull.at[n, i, 1 - k], plan.r_o + n * 2 + i)
            out_copy(n, i).wait_send()
    r_.o_out[...] = r_.ofull[0]
    r_.g_out[...] = r_.ofull[1]
    for n in range(2):
        finish_d(n)
        finish_h(n)
    for o, device, core in group:
        rc(r_.x_in.at[:, core], x_dst(core), plan.s_x + o, plan.r_x, device).wait_send()
        rc(r_.c_in.at[:, core], c_dst(core), plan.s_c + o, plan.r_c, device).wait_send()
        dpack_copy(o).wait_send()
        for n in range(4):
            low_copy(n, o).wait_send()

    for b in range(2):
        hpack_each(b, sent)
    c_relay.wait_send()
    stat_copy.wait_send()
    for t in range(4):
        finish_weights(t)
    for i in range(2):
        wait_send(r_.n1.at[i, k], plan.s_n1 + i)
        wait_send(r_.n2.at[i, k], plan.s_n2 + i)
        wait_send(r_.gb.at[i, k], plan.s_gb + i)
        for which in range(4):
            core_copy(which, i).wait_send()
            y_copy(which, i).wait_send()


def spread_kernel(plan, o_in, g_in, gde, gdl, ghe, ghl, *outs):
    o_out, g_out, qd, qu, od, ou, fd, fu, sd, su = outs
    o_out[...] = o_in[...]
    g_out[...] = g_in[...]
    for ref in (qd, qu, od, ou, fd, fu, sd, su):
        ref[...] = jnp.zeros_like(ref)

    def add(n, _):
        a, b = lax.div(n, 4), lax.rem(n, 4)
        label = jnp.max(gde[a, b, 2 * RANK : 3 * RANK, 0:128].astype(F32)).astype(jnp.int32)

        def place(out, part, first):
            out[label] += part[a, b, first * RANK : (first + 1) * RANK, :].astype(F32)

        for p in range(3):
            place(qd.at[p], gdl, p)
            place(qu.at[p], ghl, p)
        place(ou, gdl, 3)
        place(od, ghl, 3)
        place(fd, gde, 0)
        place(su, gde, 1)
        place(fu, ghe, 0)
        place(sd, ghe, 1)
        return 0

    lax.fori_loop(0, plan.images, add, 0)


def shards(
    mesh, images_in, adapter_id, valid_mask, ln1_gain, ln1_bias, qkv_weight, qv_bias, out_weight, out_bias,
    ln2_gain, ln2_bias, fc1_weight, fc1_bias, fc2_weight, fc2_bias, qkv_down, qkv_up, out_down,
    out_up, fc1_down, fc1_up, fc2_down, fc2_up, out_cotangent,
):
    images, tokens, dl = images_in.shape
    assert images == 1
    hl, fl = out_weight.shape[0], fc1_weight.shape[1]
    plan = Plan(mesh, tokens, dl, hl, fl)
    half = plan.half
    scratch = plan.scratch()
    flip = lambda factor: jnp.swapaxes(factor, -1, -2)
    operands = (
        adapter_id, valid_mask, images_in.reshape(2, 2, half, dl),
        out_cotangent.reshape(2, 2, half, dl), qkv_weight, out_weight, fc1_weight, fc2_weight,
        ln1_gain, ln1_bias, out_bias, ln2_gain, ln2_bias, fc2_bias, qv_bias, fc1_bias,
        flip(qkv_down), qkv_up, flip(out_down), out_up, flip(fc1_down), fc1_up,
        flip(fc2_down), fc2_up,
    )
    in_vmem = pl.BlockSpec(memory_space=VM)
    anywhere = pl.BlockSpec(memory_space=pl.ANY)
    specs = (
        [pl.BlockSpec(memory_space=pltpu.SMEM), in_vmem] + [anywhere] * 6 + [in_vmem] * 16
    )
    groups, cols = plan.groups, plan.cols
    grads = [
        jax.ShapeDtypeStruct(lead + scratch[name].shape, BF16)
        for lead, name in (
            ((groups, cols), "gde"), ((groups, cols), "gdl"),
            ((groups, 2, 2), "ghe"), ((groups, 2, 2), "ghl"),
        )
    ]
    token_shape = jax.ShapeDtypeStruct((2, 2, half, dl), BF16)
    results = pl.pallas_call(
        functools.partial(block_kernel, plan, tuple(scratch)),
        out_shape=[token_shape, token_shape] + grads,
        in_specs=specs,
        out_specs=[in_vmem, in_vmem] + [anywhere] * 4,
        scratch_shapes=list(scratch.values()),
        compiler_params=pltpu.CompilerParams(
            collective_id=0, has_side_effects=True, vmem_limit_bytes=60 * 2**20
        ),
    )(*operands)

    f32 = lambda *shape: jax.ShapeDtypeStruct(shape, F32)
    token_out = jax.ShapeDtypeStruct((1, tokens, dl), BF16)
    outs = pl.pallas_call(
        functools.partial(spread_kernel, plan),
        out_shape=[
            token_out, token_out, f32(3, ADAPTERS, RANK, dl), f32(3, ADAPTERS, RANK, hl),
            f32(ADAPTERS, RANK, hl), f32(ADAPTERS, RANK, dl), f32(ADAPTERS, RANK, dl),
            f32(ADAPTERS, RANK, fl), f32(ADAPTERS, RANK, fl), f32(ADAPTERS, RANK, dl),
        ],
        in_specs=[in_vmem] * 6,
        out_specs=[in_vmem] * 10,
    )(
        results[0].reshape(1, tokens, dl), results[1].reshape(1, tokens, dl), *results[2:4],
        *(part.reshape((groups, cols) + part.shape[3:]) for part in results[4:]),
    )
    block_out, grad_input, qd, qu, od, ou, fd, fu, sd, su = outs
    return block_out, grad_input, flip(qd), qu, flip(od), ou, flip(fd), fu, flip(sd), su


def solution(mesh):
    placed = (
        P(("dp", "col"), None, "row"),
        P("dp"),
        P("dp", None),
        P("row"),
        P("row"),
        P(None, "row", "col"),
        P(None, "col"),
        P("col", "row"),
        P("row"),
        P("row"),
        P("row"),
        P("row", "col"),
        P("col"),
        P("col", "row"),
        P("row"),
        P(None, None, "row", None),
        P(None, None, None, "col"),
        P(None, "col", None),
        P(None, None, "row"),
        P(None, "row", None),
        P(None, None, "col"),
        P(None, "col", None),
        P(None, None, "row"),
        P(("dp", "col"), None, "row"),
    )
    return jax.shard_map(
        functools.partial(shards, mesh),
        mesh=mesh,
        in_specs=placed,
        out_specs=(
            P(("dp", "col"), None, "row"),
            P(("dp", "col"), None, "row"),
            P(None, None, "row", None),
            P(None, None, None, "col"),
            P(None, "col", None),
            P(None, None, "row"),
            P(None, "row", None),
            P(None, None, "col"),
            P(None, "col", None),
            P(None, None, "row"),
        ),
        check_vma=False,
    )
```

time: 1070 us -> 161 us (0.15); the launches traced: 1060 us -> 160 us
  waiting for transfers between devices: 825 us -> 0 us
  Pallas kernels: 0 us -> 159 us
  matrix products: 88.7 us -> 0 us
  other arithmetic: 55.6 us -> 0 us
  local copies, waits for them, and re-layouts: 41.7 us -> 0 us
  blocking collectives: 28.1 us -> 0 us
  between operations: 16.2 us -> 0.66 us
    reduce_scatter x8 -> x0, waiting for transfers between devices: 467 us -> none  [the longest x4 300 us: into_rows(): lax.psum_scatter(term(jnp.int32(0), share * lax.axis_size('row')), 'row',...]
    all_gather x8 -> x0, waiting for transfers between devices: 229 us -> none  [the longest x4 125 us: into_columns(): lax.all_gather(inputs, 'row', axis=0, tiled=True)]
    pallas_call x0 -> x2, Pallas kernels: none -> 159 us  [the longest x1 155 us: shards(): pl.pallas_call(functools.partial(block_kernel, plan, tuple(scratch)), out...]
    psum x2 -> x0, waiting for transfers between devices: 127 us -> none  [the longest x1 79.3 us: grid_program(): lax.psum((qkv_down_part, out_up_part, fc1_down_part, fc2_up_part), ('dp',...]
    dot_general x38 -> x0, matrix products: 88.7 us -> none  [the longest x8 25.4 us: project(): jnp.einsum('nskc,kcm->nsm', inputs, weights, preferred_element_type=jnp.f...]
    concatenate x8 -> x0, other arithmetic: 40.5 us -> none  [project(): jnp.concatenate([dense_part, rank_part.reshape(rank_part.shape[:2] + (-1,...]
    psum x4 -> x0, blocking collectives: 28.1 us -> none  [row_totals(): return lax.psum((first, second), 'row')]
    unnamed x197 -> x0, local copies, waits for them, and re-layouts: 20.1 us -> none
  transfers between devices with their start and end apart: 18 -> 0, of which waited for: 18 -> 0; matrix products, arithmetic and copies ran while one was open for 8% -> 0% of each run, Pallas kernels for 0% -> 0%
where the time goes in v1:
time: 161 us; the launch traced here: 160 us
  Pallas kernels  159 us (99%)
    pallas_call x1, Pallas kernels, shards(): pl.pallas_call(functools.partial(block_kernel, plan, tuple(scratch)), out...  155 us
    pallas_call x1, Pallas kernels, shards(): pl.pallas_call(functools.partial(spread_kernel, plan), out_shape=[token_o...  4.3 us

profile of v1, /device:TPU:0, one launch (start us, length us, event | category | flops | bytes accessed | tf_op | source)
XLA Modules:
  0.0 159.8 jit_solution(13241385210000980590)
XLA Ops:
  0.7 154.8 %shard_map.303 = (bf16[2,2,160,256]{3,2,1,0:T(8,128)(2,1)}, bf16[2,2,160,256]{3,2,1,0:T(8,128)(2,1)}, bf16[2,4,48,256]{3,2,1,0:T(8,128)(2,1)}, bf16[2,4,64,256]{...) custom-call(s32[4]{0:T(128)} %refs_0_.1, s32[4,640]{1,0:T(4,128)} %refs_1_.1, ...), custom_call_target="tpu_custom_call" | custom-call | tf_op jit(solution)/shard_map/pallas_call | solution.py:1106
  155.5 4.3 %shard_map.304 = (bf16[1,640,256]{2,1,0:T(8,128)(2,1)}, bf16[1,640,256]{2,1,0:T(8,128)(2,1)}, f32[3,8,16,256]{3,2,1,0:T(8,128)}, f32[3,8,16,256]{3,2,1,0:T(8,128...) custom-call(bf16[1,640,256]{2,1,0:T(8,128)(2,1)} %bitcast.17, ...), custom_call_target="tpu_custom_call" | custom-call | tf_op jit(solution)/shard_map/pallas_call | solution.py:1119

commit v2 on v1

--- a/solution.py
+++ b/solution.py
@@ -78,7 +78,7 @@
         self.s_cc, self.r_cc = s.take(), r.take()
         pieces = sum(PIECES)
         self.s_w, self.r_w = s.take(6 * pieces), r.take(16 * pieces)
-        self.s_f, self.s_r = s.take(8 * pieces), s.take(8 * pieces)
+        self.s_f = s.take(8 * pieces)
         self.s_yx, self.r_yx = s.take(4), r.take(4)
         self.s_in, self.r_in = s.take(8), r.take(8)
         self.s_dp, self.r_dp = s.take(4), r.take(4)
@@ -248,17 +248,20 @@
         return pl.ds(aligned(start, size), size)
 
     def cut(ref, t, first, lead=(), m=None, h=None):
+        rows = (dl, hl // 2, dl, fl // 2)[t]
+        start = 0 if t in (0, 2) else first * rows
+        if m is not None:
+            rows = rows // PIECES[t]
+            start = start + m * rows
+        if h is not None:
+            rows = rows // 2
+            start = start + h * rows
+        rows = span(start, rows)
         if t == 0:
-            rows = slice(None) if h is None else span(h * (dl // 2), dl // 2)
             return ref.at[lead + (slice(None), rows, span(first * (hl // 2), hl // 2))]
         if t == 2:
-            rows = slice(None) if h is None else span((2 * h + m) * (dl // 4), dl // 4)
             return ref.at[lead + (rows, span(first * (fl // 2), fl // 2))]
-        size = (hl if t == 1 else fl) // 2
-        if h is None:
-            return ref.at[lead + (span(first * size, size), slice(None))]
-        step = size // (2 * PIECES[t])
-        return ref.at[lead + (span(first * size + (2 * m + h) * step, step), slice(None))]
+        return ref.at[lead + (rows, slice(None))]
 
     def piece(t, m):
         return sum(PIECES[:t]) + m
@@ -272,14 +275,16 @@
     def turn_weights(t):
         return rc(cut(w_in[t], t, 1 - y), w_at[t], plan.s_yx + t, plan.r_yx + t, twin_y)
 
-    targets = (3 - z, lax.rem(2 + 3 * z, 5), 1 + lax.div(z, 3))
-    three = lax.rem(z, 3) == 0
+    beyond = (3 * (1 - kd), 1 + (1 - kd))
+    beside = z + 1 - 2 * e_own
 
     def push_copy(t, m, which, i):
         n, s = piece(t, m), (r, r_other)[which]
+        h = None if i == 2 else hx
+        place = n * 16 + s * 4 + e_own * 2 + (0 if i == 2 else hx)
         return rc(
-            source(t, which, m, hx), slot(t, s, e_own, m, hx), plan.s_w + n * 6 + which * 3 + i,
-            plan.r_w + n * 16 + s * 4 + e_own * 2 + hx, (x, 2 * y + kd, targets[i]),
+            source(t, which, m, h), slot(t, s, e_own, m, h), plan.s_w + n * 6 + which * 3 + i,
+            plan.r_w + place, (x, 2 * y + kd, (beyond + (beside,))[i]),
         )
 
     def own_weights(t, which):
@@ -296,52 +301,36 @@
         if which:
             turn_weights(t).wait_recv()
         for m in range(PIECES[t]):
-            push_copy(t, m, which, 0).start()
-            push_copy(t, m, which, 1).start()
-            pl.when(three)(lambda: push_copy(t, m, which, 2).start())
+            for i in range(3):
+                push_copy(t, m, which, i).start()
         pl.when(keeps)(lambda: own_weights(t, which).start())
         near = near_copy(t, which, (r, r_other)[which])
         pl.when(jnp.logical_not(keeps))(lambda: near.start())
 
     def arrived(t, m, s, e, h):
-        n = piece(t, m)
-        wait_recv(slot(t, s, e, m, h), plan.r_w + n * 16 + s * 4 + e * 2 + h)
-
-    def pass_copy(t, m, s, e, base, device):
+        wait_recv(
+            slot(t, s, e, m, h),
+            plan.r_w + piece(t, m) * 16 + s * 4 + e * 2 + (0 if h is None else h),
+        )
+
+    def over_x(t, m, s, e):
         n, part = piece(t, m), slot(t, s, e, m, hx)
         return rc(
-            part, part, base + n * 8 + s * 2 + e, plan.r_w + n * 16 + s * 4 + e * 2 + hx, device
+            part, part, plan.s_f + n * 8 + s * 2 + e, plan.r_w + n * 16 + s * 4 + e * 2 + hx, twin_x
         )
-
-    def over_x(t, m, s, e):
-        return pass_copy(t, m, s, e, plan.s_f, twin_x)
-
-    def over_z(t, m, s, e):
-        return pass_copy(t, m, s, e, plan.s_r, (x, r, 3 * lax.rem(z + 1, 2)))
-
-    def passes_on(e):
-        return 2 * k + e + z == 3
 
     def foreign(e):
         return 2 * k + e != z
 
-    middle = lax.rem(z + 1, 4) >= 2
-
     def forward_weights(t, m, which, part):
-        e = lax.rem(z + 1 + part, 2)
+        e = lax.rem(kd + part, 2)
         lane = 2 * (y, 1 - y)[which]
 
-        @pl.when(foreign(e))
+        @pl.when(jnp.logical_not(keeps))
         def _():
             for core in range(2):
-                s = lane + core
-                arrived(t, m, s, e, hx)
-
-                @pl.when(jnp.logical_and(middle, passes_on(e)))
-                def _():
-                    over_z(t, m, s, e).start()
-
-                over_x(t, m, s, e).start()
+                arrived(t, m, lane + core, e, hx)
+                over_x(t, m, lane + core, e).start()
 
     pending = [
         (t, m, which, part)
@@ -353,15 +342,18 @@
             forward_weights(*pending.pop(0))
 
     def wait_piece(t, m, e):
-        @pl.when(foreign(e))
+        for s in range(4):
+            pl.when(jnp.logical_not(keeps))(lambda: arrived(t, m, s, e, 1 - hx))
+
+        @pl.when(jnp.logical_and(keeps, foreign(e)))
         def _():
             for s in range(4):
-                arrived(t, m, s, e, 1 - hx)
+                arrived(t, m, s, e, None)
 
         if m > 0:
             return
 
-        @pl.when(jnp.logical_not(foreign(e)))
+        @pl.when(jnp.logical_and(keeps, jnp.logical_not(foreign(e))))
         def _():
             for which in range(2):
                 own_weights(t, which).wait()
@@ -376,20 +368,16 @@
         turn_weights(t).wait_send()
         for which in range(2):
             for m in range(PIECES[t]):
-                push_copy(t, m, which, 0).wait_send()
-                push_copy(t, m, which, 1).wait_send()
-                pl.when(three)(lambda: push_copy(t, m, which, 2).wait_send())
+                for i in range(3):
+                    push_copy(t, m, which, i).wait_send()
             near = near_copy(t, which, r)
             pl.when(jnp.logical_not(keeps))(lambda: near.wait_send())
-        for m in range(PIECES[t]):
-            for e in range(2):
-                @pl.when(foreign(e))
-                def _():
+
+        @pl.when(jnp.logical_not(keeps))
+        def _():
+            for m in range(PIECES[t]):
+                for e in range(2):
                     for s in range(4):
-                        @pl.when(jnp.logical_and(middle, passes_on(e)))
-                        def _():
-                            over_z(t, m, s, e).wait_send()
-
                         over_x(t, m, s, e).wait_send()
 
     turn_weights(0).start()
@@ -931,6 +919,13 @@
 
     project_back(0)
     share_low(3, nt(up_block, r_.gqkv[...]))
+    up_grad = jnp.zeros((3 * RANK, hl), F32)
+    for p in range(3):
+        product = tn(all_rows(r_.lowq), r_.gqkv[:, p * hl : (p + 1) * hl])
+        up_grad = up_grad + jnp.where(row_block == p, product, 0.0)
+    r_.ghl[0 : 3 * RANK] = up_grad.astype(BF16)
+    r_.ghl[3 * RANK : 4 * RANK] = tn(all_rows(r_.glowo), all_rows(r_.ctx)).astype(BF16)
+    turn_h(1)
     project_back(1)
     lane = lax.broadcasted_iota(jnp.int32, (STEP, 128), 1)
     r_.stat[...] = jnp.zeros_like(r_.stat)
@@ -947,22 +942,16 @@
         return one
 
     chip_sum(3, 0, input_sums(0))
+    start_h(1)
     chip_sum(3, 1, input_sums(1))
     r_.stx[...] = r_.stat[...].T[0:8]
     stat_copy = rc(r_.stx, r_.sty, plan.s_st, plan.r_st, twin_y)
     stat_copy.start()
     y_copy(3, 1).start()
-    up_grad = jnp.zeros((3 * RANK, hl), F32)
-    for p in range(3):
-        product = tn(all_rows(r_.lowq), r_.gqkv[:, p * hl : (p + 1) * hl])
-        up_grad = up_grad + jnp.where(row_block == p, product, 0.0)
-    r_.ghl[0 : 3 * RANK] = up_grad.astype(BF16)
-    r_.ghl[3 * RANK : 4 * RANK] = tn(all_rows(r_.glowo), all_rows(r_.ctx)).astype(BF16)
-    turn_h(1)
     r_.gdl[3 * RANK : 4 * RANK] = nn(total_low(0), my_slice(r_.gb)).astype(BF16)
     r_.gdl[0 : 3 * RANK] = nn(total_low(3), my_slice(r_.n1)).astype(BF16)
     start_d(1)
-    start_h(1)
+    spread_h(1)
 
     def out_copy(n, i):
         slot = plan.s_o + n * 2 + i, plan.r_o + n * 2 + i
@@ -979,8 +968,6 @@
 
     bias_half = half_vector(fc2_bias)
     for i in range(2):
-        if i == 1:
-            spread_h(1)
         y_copy(2, i).wait_recv()
 
         def last_sum(rows, i=i):

time: 161 us -> 150 us (0.932)
  Pallas kernels: 159 us -> 149 us
    pallas_call x1, Pallas kernels: 155 us -> 145 us  [shards(): pl.pallas_call(functools.partial(block_kernel, plan, tuple(scratch)), out...]
where the time goes in v2:
time: 150 us
  Pallas kernels  149 us (99%)
    pallas_call x1, Pallas kernels, shards(): pl.pallas_call(functools.partial(block_kernel, plan, tuple(scratch)), out...  145 us
    pallas_call x1, Pallas kernels, shards(): pl.pallas_call(functools.partial(spread_kernel, plan), out_shape=[token_o...  4.3 us

profile of v2, /device:TPU:0, one launch (start us, length us, event | category | flops | bytes accessed | tf_op | source)
XLA Modules:
  0.0 149.8 jit_solution(3740218576429357617)
XLA Ops:
  0.7 144.9 %shard_map.303 = (bf16[2,2,160,256]{3,2,1,0:T(8,128)(2,1)}, bf16[2,2,160,256]{3,2,1,0:T(8,128)(2,1)}, bf16[2,4,48,256]{3,2,1,0:T(8,128)(2,1)}, bf16[2,4,64,256]{...) custom-call(s32[4]{0:T(128)} %refs_0_.1, s32[4,640]{1,0:T(4,128)} %refs_1_.1, ...), custom_call_target="tpu_custom_call" | custom-call | tf_op jit(solution)/shard_map/pallas_call | solution.py:1093
  145.5 4.3 %shard_map.304 = (bf16[1,640,256]{2,1,0:T(8,128)(2,1)}, bf16[1,640,256]{2,1,0:T(8,128)(2,1)}, f32[3,8,16,256]{3,2,1,0:T(8,128)}, f32[3,8,16,256]{3,2,1,0:T(8,128...) custom-call(bf16[1,640,256]{2,1,0:T(8,128)(2,1)} %bitcast.17, ...), custom_call_target="tpu_custom_call" | custom-call | tf_op jit(solution)/shard_map/pallas_call | solution.py:1106

commit v3 on v2

--- a/solution.py
+++ b/solution.py
@@ -21,6 +21,7 @@
 VM = pltpu.VMEM
 STEP = 32
 PIECES = (1, 1, 2, 2)
+RELAYED = 1
 
 
 def nn(a, b):
@@ -78,7 +79,7 @@
         self.s_cc, self.r_cc = s.take(), r.take()
         pieces = sum(PIECES)
         self.s_w, self.r_w = s.take(6 * pieces), r.take(16 * pieces)
-        self.s_f = s.take(8 * pieces)
+        self.s_f, self.s_r = s.take(8 * pieces), s.take(8 * pieces)
         self.s_yx, self.r_yx = s.take(4), r.take(4)
         self.s_in, self.r_in = s.take(8), r.take(8)
         self.s_dp, self.r_dp = s.take(4), r.take(4)
@@ -94,6 +95,7 @@
         self.s_gd, self.r_gd = s.take(2 * self.images), r.take(2 * self.images)
         self.s_gh, self.r_gh = s.take(2 * (self.groups + 2)), r.take(2 * (self.groups + 2))
         self.s_tr, self.r_tr = s.take(4), r.take(4)
+        self.s_ld = s.take(8)
         self.sends, self.receives = s.used, r.used
 
     def scratch(self):
@@ -122,6 +124,14 @@
             "dfull": VM((4, 7 * RANK, self.dl), BF16),
             "ha": VM((5 * RANK, self.hl), BF16),
             "hb": VM((3 * RANK, self.fl), BF16),
+            "qd_in": VM((3, ADAPTERS, RANK, self.dl), BF16),
+            "qu_in": VM((3, ADAPTERS, RANK, self.hl), BF16),
+            "od_in": VM((ADAPTERS, RANK, self.hl), BF16),
+            "ou_in": VM((ADAPTERS, RANK, self.dl), BF16),
+            "fd_in": VM((ADAPTERS, RANK, self.dl), BF16),
+            "fu_in": VM((ADAPTERS, RANK, self.fl), BF16),
+            "sd_in": VM((ADAPTERS, RANK, self.fl), BF16),
+            "su_in": VM((ADAPTERS, RANK, self.dl), BF16),
             "m1": own(F32, 1),
             "i1": own(F32, 1),
             "m2": own(F32, 1),
@@ -144,6 +154,7 @@
             "act": VM((2, pair, self.fl), BF16),
             "slope": VM((2, pair, self.fl), F32),
             "gh": VM((2, pair, self.fl), BF16),
+            "gsum": VM((2, pair, width), F32),
             "mixed": own(F32, width),
             "gmix": own(F32, width),
             "psum": VM((4, 2, 2, half, width), BF16),
@@ -169,7 +180,7 @@
 
 INPUTS = (
     "labels", "mask", "x_in", "c_in", "wq_in", "wo_in", "w1_in", "w2_in", "g1_in", "b1_in", "ob_in", "g2_in", "b2_in", "sb_in", "qb_in", "fb_in",
-    "qd_in", "qu_in", "od_in", "ou_in", "fd_in", "fu_in", "sd_in", "su_in",
+    "qd_far", "qu_far", "od_far", "ou_far", "fd_far", "fu_far", "sd_far", "su_far",
 )
 OUTPUTS = ("o_out", "g_out", "gde_all", "gdl_all", "ghe_all", "ghl_all")
 
@@ -203,6 +214,17 @@
     def wait_send(src, send):
         rc(src, src, send, 0, twin_k).wait_send()
 
+    loads = [
+        pltpu.make_async_copy(far, near, ss.at[plan.s_ld + n])
+        for n, (far, near) in enumerate((
+            (r_.qd_far, r_.qd_in), (r_.qu_far, r_.qu_in), (r_.od_far, r_.od_in),
+            (r_.ou_far, r_.ou_in), (r_.fd_far, r_.fd_in), (r_.fu_far, r_.fu_in),
+            (r_.sd_far, r_.sd_in), (r_.su_far, r_.su_in),
+        ))
+    ]
+    for load in loads:
+        load.start()
+
     barrier = pltpu.get_barrier_semaphore()
     total = plan.groups * 16
     place = (x * 4 + r) * 4 + z
@@ -278,10 +300,14 @@
     beyond = (3 * (1 - kd), 1 + (1 - kd))
     beside = z + 1 - 2 * e_own
 
+    def goals(t):
+        return (1, 2) if t < RELAYED else (0, 1, 2)
+
     def push_copy(t, m, which, i):
         n, s = piece(t, m), (r, r_other)[which]
-        h = None if i == 2 else hx
-        place = n * 16 + s * 4 + e_own * 2 + (0 if i == 2 else hx)
+        whole = i == 2 and t >= RELAYED
+        h = None if whole else hx
+        place = n * 16 + s * 4 + e_own * 2 + (0 if whole else hx)
         return rc(
             source(t, which, m, h), slot(t, s, e_own, m, h), plan.s_w + n * 6 + which * 3 + i,
             plan.r_w + place, (x, 2 * y + kd, (beyond + (beside,))[i]),
@@ -297,15 +323,23 @@
         place = t * 2 + which
         return rc(source(t, which), slot(t, s, e_own), plan.s_in + place, plan.r_in + place, twin_k)
 
-    def push_weights(t, which):
+    def push_far(t, which):
         if which:
             turn_weights(t).wait_recv()
         for m in range(PIECES[t]):
-            for i in range(3):
+            for i in goals(t)[:-1]:
                 push_copy(t, m, which, i).start()
+
+    def push_near(t, which):
+        for m in range(PIECES[t]):
+            push_copy(t, m, which, 2).start()
         pl.when(keeps)(lambda: own_weights(t, which).start())
         near = near_copy(t, which, (r, r_other)[which])
         pl.when(jnp.logical_not(keeps))(lambda: near.start())
+
+    def push_weights(t, which):
+        push_far(t, which)
+        push_near(t, which)
 
     def arrived(t, m, s, e, h):
         wait_recv(
@@ -313,23 +347,36 @@
             plan.r_w + piece(t, m) * 16 + s * 4 + e * 2 + (0 if h is None else h),
         )
 
-    def over_x(t, m, s, e):
+    def pass_copy(t, m, s, e, base, device):
         n, part = piece(t, m), slot(t, s, e, m, hx)
         return rc(
-            part, part, plan.s_f + n * 8 + s * 2 + e, plan.r_w + n * 16 + s * 4 + e * 2 + hx, twin_x
+            part, part, base + n * 8 + s * 2 + e, plan.r_w + n * 16 + s * 4 + e * 2 + hx, device
         )
+
+    def over_x(t, m, s, e):
+        return pass_copy(t, m, s, e, plan.s_f, twin_x)
+
+    def over_z(t, m, s, e):
+        return pass_copy(t, m, s, e, plan.s_r, (x, r, 3 * kd))
 
     def foreign(e):
         return 2 * k + e != z
+
+    relays = jnp.logical_and(jnp.logical_not(keeps), jnp.logical_or(z == 1, z == 2))
+
+    def halved(t, e):
+        return foreign(e) if t < RELAYED else jnp.logical_not(keeps)
 
     def forward_weights(t, m, which, part):
         e = lax.rem(kd + part, 2)
         lane = 2 * (y, 1 - y)[which]
 
-        @pl.when(jnp.logical_not(keeps))
+        @pl.when(halved(t, e))
         def _():
             for core in range(2):
                 arrived(t, m, lane + core, e, hx)
+                if t < RELAYED:
+                    pl.when(relays)(lambda: over_z(t, m, lane + core, e).start())
                 over_x(t, m, lane + core, e).start()
 
     pending = [
@@ -342,13 +389,17 @@
             forward_weights(*pending.pop(0))
 
     def wait_piece(t, m, e):
-        for s in range(4):
-            pl.when(jnp.logical_not(keeps))(lambda: arrived(t, m, s, e, 1 - hx))
-
-        @pl.when(jnp.logical_and(keeps, foreign(e)))
+        @pl.when(halved(t, e))
         def _():
             for s in range(4):
-                arrived(t, m, s, e, None)
+                arrived(t, m, s, e, 1 - hx)
+
+        if t >= RELAYED:
+
+            @pl.when(jnp.logical_and(keeps, foreign(e)))
+            def _():
+                for s in range(4):
+                    arrived(t, m, s, e, None)
 
         if m > 0:
             return
@@ -368,16 +419,19 @@
         turn_weights(t).wait_send()
         for which in range(2):
             for m in range(PIECES[t]):
-                for i in range(3):
+                for i in goals(t):
                     push_copy(t, m, which, i).wait_send()
             near = near_copy(t, which, r)
             pl.when(jnp.logical_not(keeps))(lambda: near.wait_send())
 
-        @pl.when(jnp.logical_not(keeps))
-        def _():
-            for m in range(PIECES[t]):
-                for e in range(2):
+        for m in range(PIECES[t]):
+            for e in range(2):
+
+                @pl.when(halved(t, e))
+                def _():
                     for s in range(4):
+                        if t < RELAYED:
+                            pl.when(relays)(lambda: over_z(t, m, s, e).wait_send())
                         over_x(t, m, s, e).wait_send()
 
     turn_weights(0).start()
@@ -387,6 +441,8 @@
     turn_weights(2).start()
     turn_weights(3).start()
 
+    for load in loads:
+        load.wait()
     mine = r_.labels[z]
     theirs = r_.labels[r]
     for p in range(3):
@@ -486,7 +542,7 @@
     forward_weights(0, 0, 0, 0)
     forward_weights(0, 0, 0, 1)
     push_weights(1, 1)
-    push_weights(2, 0)
+    push_far(2, 0)
     forward_weights(0, 0, 1, 0)
     forward_weights(0, 0, 1, 1)
     for o in (1, 2, 3):
@@ -506,10 +562,12 @@
 
     forward_weights(1, 0, 0, 0)
     forward_weights(1, 0, 0, 1)
-    push_weights(2, 1)
-    push_weights(3, 0)
+    push_far(2, 1)
     forward_weights(1, 0, 1, 0)
     forward_weights(1, 0, 1, 1)
+    push_near(2, 0)
+    push_near(2, 1)
+    push_weights(3, 0)
     wait_hpack()
     for i in range(2):
         twin_wait(r_.n1, i, plan.r_n1)
@@ -671,10 +729,20 @@
         grad = grad + nn(r_.glow2[i], r_.hb[RANK : 2 * RANK, cols])
         r_.gh[i, :, cols] = (grad * r_.slope[i, :, cols]).astype(BF16)
 
+    def gh_part(ref, m):
+        size = fl // 4
+        return jnp.concatenate([ref[..., c * size : (c + 1) * size] for c in (m, 2 + m)], axis=1)
+
+    def hidden_early(i):
+        for s in range(4):
+            r_.gsum[i, :, s * dl : (s + 1) * dl] = nt(gh_part(r_.gh.at[i], 0), gh_part(r_.w1.at[s], 0))
+
     def hidden_back(i):
         low = nt(r_.gh[i], r_.hb[0:RANK, :]).astype(BF16)
         for s in range(4):
-            value = nt(r_.gh[i], r_.w1[s]) + nn(low, r_.dfull[s, 4 * RANK : 5 * RANK, :])
+            value = r_.gsum[i, :, s * dl : (s + 1) * dl]
+            value = value + nt(gh_part(r_.gh.at[i], 1), gh_part(r_.w1.at[s], 1))
+            value = value + nn(low, r_.dfull[s, 4 * RANK : 5 * RANK, :])
             keep_sum(1, i, s, value)
         core_copy(1, i).start()
 
@@ -822,14 +890,21 @@
 
     low_grads(0)
     low_grads(1)
+    serve(4)
+    for e in range(2):
+        wait_piece(3, 0, e)
+        hidden_grads(2 * e, 0)
+        hidden_grads(2 * e, 1)
     serve(16)
-    for m, e in ((0, 0), (0, 1), (1, 0), (1, 1)):
-        f = 2 * e + m
-        wait_piece(3, m, e)
-        hidden_grads(f, 0)
-        if f == 3:
-            hidden_back(0)
-        hidden_grads(f, 1)
+    hidden_early(0)
+    hidden_early(1)
+    wait_piece(3, 1, 0)
+    hidden_grads(1, 0)
+    wait_piece(3, 1, 1)
+    hidden_grads(3, 0)
+    hidden_back(0)
+    hidden_grads(1, 1)
+    hidden_grads(3, 1)
     chip_sum(1, 0)
     hidden_back(1)
     chip_sum(1, 1)
@@ -900,9 +975,8 @@
     r_.gde[RANK : 2 * RANK] = nn(total_low(1), my_slice(r_.cg)).astype(BF16)
     r_.gde[2 * RANK : 3 * RANK] = jnp.zeros((RANK, dl), BF16) + mine.astype(F32).astype(BF16)
     start_d(0)
+    attend_back(1)
     spread_h(0)
-    attend_back(1)
-    share_h(0)
     r_.gqkv[:, 0:hl] = jnp.concatenate([r_.gqh[h] for h in range(plan.heads)], axis=1)
     r_.gqkv[:, hl : 2 * hl] = r_.dk[...].reshape(hl, plan.tokens).T.astype(BF16)
     r_.gqkv[:, 2 * hl : 3 * hl] = r_.dv[...].reshape(hl, plan.tokens).T.astype(BF16)
@@ -942,6 +1016,7 @@
         return one
 
     chip_sum(3, 0, input_sums(0))
+    share_h(0)
     start_h(1)
     chip_sum(3, 1, input_sums(1))
     r_.stx[...] = r_.stat[...].T[0:8]
@@ -951,7 +1026,6 @@
     r_.gdl[3 * RANK : 4 * RANK] = nn(total_low(0), my_slice(r_.gb)).astype(BF16)
     r_.gdl[0 : 3 * RANK] = nn(total_low(3), my_slice(r_.n1)).astype(BF16)
     start_d(1)
-    spread_h(1)
 
     def out_copy(n, i):
         slot = plan.s_o + n * 2 + i, plan.r_o + n * 2 + i
@@ -978,11 +1052,13 @@
         out_copy(0, i).start()
 
     gain_half = half_vector(gain_one)
-    share_h(1)
+    spread_h(1)
     stat_copy.wait_recv()
     joined = r_.stx[...] + r_.sty[...]
     r_.stat[...] = jnp.concatenate([joined, jnp.zeros((120, 384), F32)], axis=0).T
     for i in range(2):
+        if i == 1:
+            share_h(1)
         y_copy(3, i).wait_recv()
 
         def last_grad(t, _, i=i):
@@ -1079,7 +1155,7 @@
     in_vmem = pl.BlockSpec(memory_space=VM)
     anywhere = pl.BlockSpec(memory_space=pl.ANY)
     specs = (
-        [pl.BlockSpec(memory_space=pltpu.SMEM), in_vmem] + [anywhere] * 6 + [in_vmem] * 16
+        [pl.BlockSpec(memory_space=pltpu.SMEM), in_vmem] + [anywhere] * 6 + [in_vmem] * 8 + [anywhere] * 8
     )
     groups, cols = plan.groups, plan.cols
     grads = [

time: 150 us -> 143 us (0.953)
  Pallas kernels: 149 us -> 141 us
    pallas_call x1, Pallas kernels: 145 us -> 137 us  [shards(): pl.pallas_call(functools.partial(block_kernel, plan, tuple(scratch)), out...]
where the time goes in v3:
time: 143 us; the launch traced here: 142 us
  Pallas kernels  141 us (99%)
    pallas_call x1, Pallas kernels, shards(): pl.pallas_call(functools.partial(block_kernel, plan, tuple(scratch)), out...  137 us
    pallas_call x1, Pallas kernels, shards(): pl.pallas_call(functools.partial(spread_kernel, plan), out_shape=[token_o...  4.3 us

profile of v3, /device:TPU:0, one launch (start us, length us, event | category | flops | bytes accessed | tf_op | source)
XLA Modules:
  0.0 141.9 jit_solution(557934679621777045)
XLA Ops:
  0.7 137.0 %shard_map.303 = (bf16[2,2,160,256]{3,2,1,0:T(8,128)(2,1)}, bf16[2,2,160,256]{3,2,1,0:T(8,128)(2,1)}, bf16[2,4,48,256]{3,2,1,0:T(8,128)(2,1)}, bf16[2,4,64,256]{...) custom-call(s32[4]{0:T(128)} %refs_0_.1, s32[4,640]{1,0:T(4,128)} %refs_1_.1, ...), custom_call_target="tpu_custom_call" | custom-call | tf_op jit(solution)/shard_map/pallas_call | solution.py:1169
  137.6 4.3 %shard_map.304 = (bf16[1,640,256]{2,1,0:T(8,128)(2,1)}, bf16[1,640,256]{2,1,0:T(8,128)(2,1)}, f32[3,8,16,256]{3,2,1,0:T(8,128)}, f32[3,8,16,256]{3,2,1,0:T(8,128...) custom-call(bf16[1,640,256]{2,1,0:T(8,128)(2,1)} %bitcast.17, ...), custom_call_target="tpu_custom_call" | custom-call | tf_op jit(solution)/shard_map/pallas_call | solution.py:1182

commit v4 on v3

--- a/solution.py
+++ b/solution.py
@@ -231,14 +231,17 @@
 
     def greet(o, _):
         t = lax.rem(place + o, total)
-        pl.semaphore_signal(
-            barrier, inc=1, device_id=(lax.div(t, 16), lax.rem(lax.div(t, 4), 4), lax.rem(t, 4)),
-            device_id_type=MESH,
-        )
+        there = (lax.div(t, 16), lax.rem(lax.div(t, 4), 4), lax.rem(t, 4))
+        met = jnp.logical_or(there[0] == x, jnp.logical_or(there[1] == r, there[2] == z))
+
+        @pl.when(met)
+        def _():
+            pl.semaphore_signal(barrier, inc=1, device_id=there, device_id_type=MESH)
+
         return 0
 
     lax.fori_loop(1, total, greet, 0)
-    pl.semaphore_wait(barrier, total - 1)
+    pl.semaphore_wait(barrier, 15 + 7 * (plan.groups - 1))
 
     my_cols = pl.ds(aligned(r * dl, dl), dl)
     group = (
@@ -676,7 +679,7 @@
     wait_tokens(r_.c_in, c_dst, plan.s_c, plan.r_c)
     c_relay = rc(r_.cg.at[:, k], r_.cg.at[:, k], plan.s_cc, plan.r_cc, twin_k)
     c_relay.start()
-    serve(4)
+    serve(6)
 
     out_bias, gain_two, bias_two, fc2_bias = (d_vector(n) for n in (2, 3, 4, 5))
 
@@ -950,8 +953,7 @@
             r_.gh_h[h, i * pair : (i + 1) * pair, :] = value[:, h * HEAD_DIM : (h + 1) * HEAD_DIM]
 
         def one(t, _):
-            h, u = lax.div(t, 2), lax.rem(t, 2)
-            rows = pl.ds(aligned(i * pair + u * half, half), half)
+            h, rows = t, slice(i * pair, (i + 1) * pair)
             grad, probs = r_.gh_h[h, rows, :], r_.probs[h, rows, :]
             inner = jnp.sum(
                 grad.astype(F32) * r_.ch[h, rows, :].astype(F32), axis=-1, keepdims=True
@@ -962,7 +964,7 @@
             r_.dv[h] += tn(grad, probs)
             return 0
 
-        lax.fori_loop(0, 2 * plan.heads, one, 0)
+        lax.fori_loop(0, plan.heads, one, 0, unroll=2)
 
     mixed_grad(0)
     r_.ghe[0:RANK] = tn(all_rows(r_.low1), all_rows(r_.gh)).astype(BF16)
@@ -1105,32 +1107,38 @@
             y_copy(which, i).wait_send()
 
 
-def spread_kernel(plan, o_in, g_in, gde, gdl, ghe, ghl, *outs):
-    o_out, g_out, qd, qu, od, ou, fd, fu, sd, su = outs
-    o_out[...] = o_in[...]
-    g_out[...] = g_in[...]
-    for ref in (qd, qu, od, ou, fd, fu, sd, su):
-        ref[...] = jnp.zeros_like(ref)
-
-    def add(n, _):
-        a, b = lax.div(n, 4), lax.rem(n, 4)
-        label = jnp.max(gde[a, b, 2 * RANK : 3 * RANK, 0:128].astype(F32)).astype(jnp.int32)
-
-        def place(out, part, first):
-            out[label] += part[a, b, first * RANK : (first + 1) * RANK, :].astype(F32)
-
-        for p in range(3):
-            place(qd.at[p], gdl, p)
-            place(qu.at[p], ghl, p)
-        place(ou, gdl, 3)
-        place(od, ghl, 3)
-        place(fd, gde, 0)
-        place(su, gde, 1)
-        place(fu, ghe, 0)
-        place(sd, ghe, 1)
-        return 0
-
-    lax.fori_loop(0, plan.images, add, 0)
+def spread_kernel(plan, o_in, g_in, gde, gdl, ghe, ghl, *refs):
+    outs, held, sems = refs[:10], refs[10:18], refs[18]
+    qd, qu, od, ou, fd, fu, sd, su = held
+    passed = [
+        pltpu.make_async_copy(o_in, outs[0], sems.at[0]),
+        pltpu.make_async_copy(g_in, outs[1], sems.at[1]),
+    ]
+    for copy in passed:
+        copy.start()
+    labels = []
+    for n in range(plan.images):
+        row = gde[n // 4, n % 4, 2 * RANK : 3 * RANK, 0:128].astype(F32)
+        labels.append(jnp.max(row).astype(jnp.int32))
+    plans = (
+        ((fu, ghe, 0), 5), ((sd, ghe, 1), 6), ((fd, gde, 0), 4), ((su, gde, 1), 7),
+        ((ou, gdl, 3), 3), ((od, ghl, 3), 2), ((qd, gdl, None), 0), ((qu, ghl, None), 1),
+    )
+    copies = []
+    for (out, source, first), place in plans:
+        out[...] = jnp.zeros_like(out)
+        for n, label in enumerate(labels):
+            for p in range(3) if first is None else (first,):
+                rows = source[n // 4, n % 4, p * RANK : (p + 1) * RANK, :].astype(F32)
+                if first is None:
+                    out[p, label] += rows
+                else:
+                    out[label] += rows
+        copy = pltpu.make_async_copy(out, outs[2 + place], sems.at[2 + place])
+        copy.start()
+        copies.append(copy)
+    for copy in passed + copies:
+        copy.wait()
 
 
 def shards(
@@ -1187,7 +1195,15 @@
             f32(ADAPTERS, RANK, fl), f32(ADAPTERS, RANK, fl), f32(ADAPTERS, RANK, dl),
         ],
         in_specs=[in_vmem] * 6,
-        out_specs=[in_vmem] * 10,
+        out_specs=[anywhere] * 10,
+        scratch_shapes=[
+            VM(shape, F32)
+            for shape in (
+                (3, ADAPTERS, RANK, dl), (3, ADAPTERS, RANK, hl), (ADAPTERS, RANK, hl),
+                (ADAPTERS, RANK, dl), (ADAPTERS, RANK, dl), (ADAPTERS, RANK, fl),
+                (ADAPTERS, RANK, fl), (ADAPTERS, RANK, dl),
+            )
+        ] + [pltpu.SemaphoreType.DMA((10,))],
     )(
         results[0].reshape(1, tokens, dl), results[1].reshape(1, tokens, dl), *results[2:4],
         *(part.reshape((groups, cols) + part.shape[3:]) for part in results[4:]),

time: 143 us -> 139 us (0.972)
  Pallas kernels: 141 us -> 138 us
    pallas_call x1, Pallas kernels: 137 us -> 134 us  [shards(): pl.pallas_call(functools.partial(block_kernel, plan, tuple(scratch)), out...]
where the time goes in v4:
time: 139 us
  Pallas kernels  138 us (99%)
    pallas_call x1, Pallas kernels, shards(): pl.pallas_call(functools.partial(block_kernel, plan, tuple(scratch)), out...  134 us
    pallas_call x1, Pallas kernels, shards(): pl.pallas_call(functools.partial(spread_kernel, plan), out_shape=[token_o...  3.23 us

profile of v4, /device:TPU:0, one launch (start us, length us, event | category | flops | bytes accessed | tf_op | source)
XLA Modules:
  0.0 138.5 jit_solution(1526241043128043232)
XLA Ops:
  0.7 134.4 %shard_map.303 = (bf16[2,2,160,256]{3,2,1,0:T(8,128)(2,1)}, bf16[2,2,160,256]{3,2,1,0:T(8,128)(2,1)}, bf16[2,4,48,256]{3,2,1,0:T(8,128)(2,1)}, bf16[2,4,64,256]{...) custom-call(s32[4]{0:T(128)} %refs_0_.1, s32[4,640]{1,0:T(4,128)} %refs_1_.1, ...), custom_call_target="tpu_custom_call" | custom-call | tf_op jit(solution)/shard_map/pallas_call | solution.py:1177
  135.1 3.2 %shard_map.304 = (bf16[1,640,256]{2,1,0:T(8,128)(2,1)}, bf16[1,640,256]{2,1,0:T(8,128)(2,1)}, f32[3,8,16,256]{3,2,1,0:T(8,128)}, f32[3,8,16,256]{3,2,1,0:T(8,128...) custom-call(bf16[1,640,256]{2,1,0:T(8,128)(2,1)} %bitcast.17, ...), custom_call_target="tpu_custom_call" | custom-call | tf_op jit(solution)/shard_map/pallas_call | solution.py:1190

commit v5 on v4

--- a/solution.py
+++ b/solution.py
@@ -609,8 +609,7 @@
 
     def attend(i, first, last):
         def one(t, _):
-            h, u = lax.div(t, 2), lax.rem(t, 2)
-            rows = pl.ds(aligned(i * pair + u * half, half), half)
+            h, rows = t, slice(i * pair, (i + 1) * pair)
             scores = nt(r_.qh[h, rows, :], r_.kh[h]) + shift
             powered = jnp.exp(scores - jnp.max(scores, axis=-1, keepdims=True))
             summed = jnp.sum(powered, axis=-1, keepdims=True)
@@ -619,7 +618,7 @@
             r_.ch[h, rows, :] = nn(probs, r_.vh[h]).astype(BF16)
             return 0
 
-        lax.fori_loop(2 * first, 2 * last, one, 0)
+        lax.fori_loop(first, last, one, 0)
         if last < plan.heads:
             return
         r_.ctx[i] = jnp.concatenate(
@@ -964,7 +963,7 @@
             r_.dv[h] += tn(grad, probs)
             return 0
 
-        lax.fori_loop(0, plan.heads, one, 0, unroll=2)
+        lax.fori_loop(0, plan.heads, one, 0, unroll=4)
 
     mixed_grad(0)
     r_.ghe[0:RANK] = tn(all_rows(r_.low1), all_rows(r_.gh)).astype(BF16)
@@ -993,8 +992,6 @@
             keep_sum(3, i, s, nt(grads, weight) + nn(low, r_.dfull[s, 0 : 3 * RANK, :]))
         core_copy(3, i).start()
 
-    project_back(0)
-    share_low(3, nt(up_block, r_.gqkv[...]))
     up_grad = jnp.zeros((3 * RANK, hl), F32)
     for p in range(3):
         product = tn(all_rows(r_.lowq), r_.gqkv[:, p * hl : (p + 1) * hl])
@@ -1002,6 +999,8 @@
     r_.ghl[0 : 3 * RANK] = up_grad.astype(BF16)
     r_.ghl[3 * RANK : 4 * RANK] = tn(all_rows(r_.glowo), all_rows(r_.ctx)).astype(BF16)
     turn_h(1)
+    project_back(0)
+    share_low(3, nt(up_block, r_.gqkv[...]))
     project_back(1)
     lane = lax.broadcasted_iota(jnp.int32, (STEP, 128), 1)
     r_.stat[...] = jnp.zeros_like(r_.stat)
@@ -1017,9 +1016,9 @@
 
         return one
 
+    start_h(1)
     chip_sum(3, 0, input_sums(0))
     share_h(0)
-    start_h(1)
     chip_sum(3, 1, input_sums(1))
     r_.stx[...] = r_.stat[...].T[0:8]
     stat_copy = rc(r_.stx, r_.sty, plan.s_st, plan.r_st, twin_y)

time: 139 us -> 139 us (level)
  no operation moved by 1% of the time
where the time goes in v5:
time: 139 us
  Pallas kernels  138 us (99%)
    pallas_call x1, Pallas kernels, shards(): pl.pallas_call(functools.partial(block_kernel, plan, tuple(scratch)), out...  135 us
    pallas_call x1, Pallas kernels, shards(): pl.pallas_call(functools.partial(spread_kernel, plan), out_shape=[token_o...  3.23 us

profile of v5, /device:TPU:0, one launch (start us, length us, event | category | flops | bytes accessed | tf_op | source)
XLA Modules:
  0.0 138.6 jit_solution(10897595403340957943)
XLA Ops:
  0.7 134.6 %shard_map.303 = (bf16[2,2,160,256]{3,2,1,0:T(8,128)(2,1)}, bf16[2,2,160,256]{3,2,1,0:T(8,128)(2,1)}, bf16[2,4,48,256]{3,2,1,0:T(8,128)(2,1)}, bf16[2,4,64,256]{...) custom-call(s32[4]{0:T(128)} %refs_0_.1, s32[4,640]{1,0:T(4,128)} %refs_1_.1, ...), custom_call_target="tpu_custom_call" | custom-call | tf_op jit(solution)/shard_map/pallas_call | solution.py:1176
  135.2 3.2 %shard_map.304 = (bf16[1,640,256]{2,1,0:T(8,128)(2,1)}, bf16[1,640,256]{2,1,0:T(8,128)(2,1)}, f32[3,8,16,256]{3,2,1,0:T(8,128)}, f32[3,8,16,256]{3,2,1,0:T(8,128...) custom-call(bf16[1,640,256]{2,1,0:T(8,128)(2,1)} %bitcast.17, ...), custom_call_target="tpu_custom_call" | custom-call | tf_op jit(solution)/shard_map/pallas_call | solution.py:1189
